TPU v7x, 32 devices: a whole 2x2x4 slice. The times are simulated.
32 devices in a mesh: sec: 2 (over x), gx: 4 (over z), az: 4 (over y, core).
Axes of the slice: x: 2, y: 2, z: 4, core: 2. Of those that a mesh axis runs over, the one named last changes fastest.
Arguments:
- les_velocity: float32 [3, 8, 64, 1024], P(None, None, 'az', ('sec', 'gx')), may hold values from -6 to 6
- les_metric: float32 [3, 8, 64, 1024], P(None, None, 'az', ('sec', 'gx')), may hold values from 0.5 to 1.5
- caa_state: float32 [4, 8, 64, 1024], P(None, None, 'az', ('sec', 'gx')), may hold values from -6 to 6
- caa_metric: float32 [3, 8, 64, 1024], P(None, None, 'az', ('sec', 'gx')), may hold values from 0.5 to 1.5
- intersection_refs: int32 [128, 4], P(('sec', 'gx')), may hold values from 0 to 7, as said below
- offsets: int32 [128], P(('sec', 'gx')), may hold values from 0 to 8
- send_list: int32 [8, 4, 8], replicated, may hold values from -1 to 15, as said below
Outputs:
- les_out: float32 [3, 8, 64, 1024], P(None, None, 'az', ('sec', 'gx'))
- caa_out: float32 [4, 8, 64, 1024], P(None, None, 'az', ('sec', 'gx'))
Inputs may be any that keep to these rules, and one draw needn't show every extreme that they name: `intersection_refs`: row j belongs to slab r = j // 16; columns 0 and 2 are slabs of r's section (0 to 3), columns 1 and 3 slots (0 to 7). Among the 32 pairs of one slab no (slab, slot) pair repeats, at most 8 name one slab and exactly 8 name some slab, the slots towards one slab are filled from 0 upward, and send_list holds a block (not -1) at every named pair. send_list[s, d, c] is a block of slab s (0 to 15) for slot c of slab d of the same section, and -1 exactly where no row of slab d names (s, c).
All inputs are finite; a program needn't handle non-finite values.
Results may differ from a plain program's by a relative error of at most 0.00081.
Values may be sent and summed in bfloat16 or wider, within the bound.
A program may use at most 64 MiB of HBM per device.

v0:
```python
import jax
import jax.numpy as jnp
import numpy as np
from jax import lax
from jax.sharding import PartitionSpec as P

LES_STEPS = 2
CAA_SUB = 4


les_step = 0.02
caa_step = 0.01
mach_number = 0.5
margin_nodes = 16


def with_halo(cells, sides, width, closed):
    for axis, dim in sides:
        count = lax.axis_size(axis)
        ends = count if closed else count - 1
        head = lax.slice_in_dim(cells, 0, width, axis=dim)
        tail = lax.slice_in_dim(cells, cells.shape[dim] - width, cells.shape[dim], axis=dim)
        cells = jnp.concatenate(
            [
                lax.ppermute(tail, axis, [(i, (i + 1) % count) for i in range(ends)]),
                cells,
                lax.ppermute(head, axis, [((i + 1) % count, i) for i in range(ends)]),
            ],
            axis=dim,
        )
    return cells


def slope_table():
    points = np.array([-1.0, -(0.2**0.5), 0.2**0.5, 1.0])
    identity = np.eye(4)
    differences = points[:, None] - points[None, :] + identity
    inverse_weights = 1.0 / np.prod(differences, axis=1)
    slope_matrix = inverse_weights[None, :] / inverse_weights[:, None] / differences
    slope_matrix = slope_matrix * (1.0 - identity)
    return slope_matrix - identity * slope_matrix.sum(axis=1)[:, None]


def line_matrix(length):
    slope_matrix = slope_table()
    result = np.zeros((length + 2, length))
    for element in range(length // 4):
        offset_node = 4 * element
        result[1 + offset_node : 5 + offset_node, offset_node : offset_node + 4] += slope_matrix.T
        result[offset_node + 1, offset_node] += 3.0
        result[offset_node, offset_node] -= 3.0
        result[offset_node + 5, offset_node + 3] += 3.0
        result[offset_node + 4, offset_node + 3] -= 3.0
    return jnp.asarray(result, jnp.float32)


def stream_pad(quantity):
    return jnp.pad(quantity, ((0, 0), (0, 0), (0, 0), (1, 1)))


def azimuth_extend(quantity):
    return with_halo(quantity, (("az", 2),), 1, True)


def radial_extend(quantity):
    return jnp.pad(quantity, ((0, 0), (1, 1), (0, 0), (0, 0)))


def stream_apply(extended, matrix):
    return jnp.einsum("cras,st->crat", extended, matrix, precision=lax.Precision.HIGHEST)


def azimuth_apply(extended, matrix):
    return jnp.einsum("cras,at->crts", extended, matrix, precision=lax.Precision.HIGHEST)


def radial_apply(extended, matrix):
    return jnp.einsum("cras,rt->ctas", extended, matrix, precision=lax.Precision.HIGHEST)


def les_rates(velocity, metric, matrices, extended):
    stacked = jnp.concatenate([extended, extended[0:1] * extended], axis=0)
    stream_slope = metric[0] * stream_apply(stacked, matrices[0])
    extended = azimuth_extend(velocity)
    stacked = jnp.concatenate([extended, extended[1:2] * extended], axis=0)
    azimuth_slope = metric[1] * azimuth_apply(stacked, matrices[1])
    extended = radial_extend(velocity)
    stacked = jnp.concatenate([extended, extended[2:3] * extended], axis=0)
    radial_slope = metric[2] * radial_apply(stacked, matrices[2])
    slopes = (stream_slope[:3], azimuth_slope[:3], radial_slope[:3])
    fluxes = (stream_slope[3:], azimuth_slope[3:], radial_slope[3:])
    omega_first = slopes[1][2] - slopes[2][1]
    omega_second = slopes[2][0] - slopes[0][2]
    omega_third = slopes[0][1] - slopes[1][0]
    lamb_vector = jnp.stack(
        [
            omega_second * velocity[2] - omega_third * velocity[1],
            omega_third * velocity[0] - omega_first * velocity[2],
            omega_first * velocity[1] - omega_second * velocity[0],
        ]
    )
    return (slopes, fluxes, lamb_vector)


def caa_rates(acoustic, metric, source, matrices, stream_fn):
    stream_slope = metric[0] * stream_apply(stream_fn(acoustic), matrices[0])
    paired = jnp.stack([acoustic[0], acoustic[2]])
    azimuth_slope = metric[1] * azimuth_apply(azimuth_extend(paired), matrices[1])
    paired = jnp.stack([acoustic[0], acoustic[3]])
    radial_slope = metric[2] * radial_apply(radial_extend(paired), matrices[2])
    return jnp.stack(
        [
            -(mach_number * stream_slope[0] + stream_slope[1] + azimuth_slope[1] + radial_slope[1]),
            -(mach_number * stream_slope[1] + stream_slope[0]) + source[0],
            -(mach_number * stream_slope[2] + azimuth_slope[0]) + source[1],
            -(mach_number * stream_slope[3] + radial_slope[0]) + source[2],
        ]
    )


def couple(lamb_vector, intersection_refs, offsets, send_list):
    rounded = lamb_vector.astype(jnp.bfloat16)
    components, radial_nodes, sector_nodes, stream_nodes = rounded.shape
    block_count = stream_nodes // 8
    packed = rounded.reshape(components, radial_nodes, sector_nodes, block_count, 8)
    packed = packed.transpose(3, 0, 1, 2, 4).reshape(block_count, -1)
    section = lax.axis_index("sec")
    own_slab = lax.axis_index("gx")
    slab_count = lax.axis_size("gx")
    gathered = lax.all_gather(packed, "gx", axis=0, tiled=True)

    def fetch_block(owner_slab, slot_index):
        local_block = send_list[section * slab_count + owner_slab, own_slab, slot_index]
        return gathered[owner_slab * block_count + local_block]

    leading = fetch_block(intersection_refs[:, 0], intersection_refs[:, 1]).astype(jnp.float32)
    trailing = fetch_block(intersection_refs[:, 2], intersection_refs[:, 3]).astype(jnp.float32)
    fraction = offsets.astype(jnp.float32)[:, None]
    blended = ((8.0 - fraction) * leading + fraction * trailing) / 8.0
    blended = blended.reshape(block_count, components, radial_nodes, sector_nodes, 8)
    return blended.transpose(1, 2, 3, 0, 4).reshape(
        components, radial_nodes, sector_nodes, stream_nodes
    )


def body(les_velocity, les_metric, caa_state, caa_metric, intersection_refs, offsets, send_list):
    radial_nodes = les_velocity.shape[1]
    sector_nodes = les_velocity.shape[2]
    stream_nodes = les_velocity.shape[3]
    matrices = (line_matrix(stream_nodes), line_matrix(sector_nodes), line_matrix(radial_nodes))
    velocity = les_velocity
    acoustic = caa_state
    wide_matrices = (line_matrix(stream_nodes + 2 * margin_nodes), matrices[1], matrices[2])
    metric_wide = with_halo(caa_metric, ((("sec", "gx"), 3),), margin_nodes, False)
    for les_round in range(LES_STEPS):
        joined = with_halo(
            jnp.concatenate([velocity, acoustic], axis=0),
            ((("sec", "gx"), 3),),
            margin_nodes,
            False,
        )
        velocity_rim = joined[:3, :, :, margin_nodes - 1 : margin_nodes + stream_nodes + 1]
        acoustic_wide = joined[3:]
        slopes, fluxes, lamb_vector = les_rates(velocity, les_metric, matrices, velocity_rim)
        source = couple(lamb_vector, intersection_refs, offsets, send_list)
        change = -0.5 * sum((fluxes[j] + velocity[j][None] * slopes[j] for j in range(3)))
        velocity = velocity + les_step * change
        source_wide = with_halo(source, ((("sec", "gx"), 3),), margin_nodes, False)
        for substep in range(CAA_SUB):
            acoustic_wide = acoustic_wide + caa_step * caa_rates(
                acoustic_wide, metric_wide, source_wide, wide_matrices, stream_pad
            )
        acoustic = acoustic_wide[:, :, :, margin_nodes : margin_nodes + stream_nodes]
    return (velocity, acoustic)


def solution(mesh):
    in_specs = (
        P(None, None, "az", ("sec", "gx")),
        P(None, None, "az", ("sec", "gx")),
        P(None, None, "az", ("sec", "gx")),
        P(None, None, "az", ("sec", "gx")),
        P(("sec", "gx"), None),
        P(("sec", "gx")),
        P(),
    )
    out_specs = (P(None, None, "az", ("sec", "gx")), P(None, None, "az", ("sec", "gx")))
    return jax.shard_map(body, mesh=mesh, in_specs=in_specs, out_specs=out_specs, check_vma=False)
```

profile of v0, /device:TPU:1, one launch (start us, length us, event | category | flops | bytes accessed | tf_op | source)
XLA Modules:
  0.0 196.9 jit_solution(7853994511271631416)
XLA Ops:
  1.6 2.7 %collective-permute-start.2 = (f32[3,8,1,128]{3,2,1,0:T(1,128)S(1)}, f32[3,8,1,128]{3,2,1,0:T(1,128)S(1)}, u32[]{:S(2)}, u32[]{:S(2)}) collective-permute-start(f32[3,8,1,128]{3,2,1,0:T(1,128)S(1)} %get-tuple-element.108), channel_id=1, source_target_pairs={{0,1},{1,2},{2,3},{3,0},{4,5},{5,6},{6,7},{7,4},{8,9},{9,10},{10,1... | collective-permute-start | bytes 36872 | tf_op jit(solution)/shard_map/ppermute | solution.py:25
  4.3 1.8 fusion.243
  6.1 4.0 %collective-permute-start.4 = (f32[3,8,16,16]{3,2,1,0:T(8,128)}, f32[3,8,16,16]{3,2,1,0:T(8,128)}, u32[]{:S(2)}, u32[]{:S(2)}) collective-permute-start(f32[3,8,16,16]{3,2,1,0:T(8,128)} %get-tuple-element.97), channel_id=1, source_target_pairs={{0,4},{4,8},{8,12},{12,16},{16,20},{20,24},{24,28},{1,5},{5,9},{9,... | collective-permute-start | bytes 73736 | tf_op jit(solution)/shard_map/ppermute | solution.py:25
  14.4 4.0 %collective-permute-start = (f32[7,8,16,16]{3,2,1,0:T(8,128)}, f32[7,8,16,16]{3,2,1,0:T(8,128)S(1)}, u32[]{:S(2)}, u32[]{:S(2)}) collective-permute-start(f32[7,8,16,16]{3,2,1,0:T(8,128)} %get-tuple-element.68), channel_id=1, source_target_pairs={{0,4},{4,8},{8,12},{12,16},{16,20},{20,24},{24,28},{1,5},{5,9},{9,... | collective-permute-start | bytes 172040 | tf_op jit(solution)/shard_map/ppermute | solution.py:25
  27.3 16.9 %collective-permute-done.1 = f32[7,8,16,16]{3,2,1,0:T(8,128)S(1)} collective-permute-done((f32[7,8,16,16]{3,2,1,0:T(8,128)S(1)}, f32[7,8,16,16]{3,2,1,0:T(8,128)S(1)}, u32[]{:S(2)}, u32[]{:S(2)}) %collective-permute-start.1) | collective-permute-done | bytes 57376 | tf_op jit(solution)/shard_map/ppermute | solution.py:27
  50.8 1.7 collective-permute-start.18
  54.3 11.4 %all_gather.6 = bf16[64,3072]{1,0:T(8,128)(2,1)S(1)} all-gather(bf16[16,3072]{1,0:T(8,128)(2,1)S(1)} %copy.47), channel_id=1, replica_groups=mesh['sec'=2,'gx'=4,'az'=4] {'gx'}, dimensions={0}, use_global_device_ids=true | all-gather | bytes 491520 | tf_op jit(solution)/shard_map/all_gather | solution.py:130
  69.2 1.4 copy.49
  70.6 2.9 %multiply_bitcast_fusion.1 = f32[3,8,16,16,8]{3,4,2,1,0:T(8,128)} fusion(f32[16,3,8,16,8]{0,4,3,2,1:T(8,128)} %bitcast.179, f32[16,3,8,16,8]{0,4,3,2,1:T(8,128)S(1)} %bitcast.178, f32[16]{0:T(128)S(1)} %copy-done.34, f32[16]{0:T(128)S(1)} %copy-done.33), kind=kLoop, calls=%fused_computation.7 | loop fusion | flops 196608 | bytes 589952 | tf_op jit(solution)/shard_map/transpose | solution.py:141
  73.5 2.0 %copy.50 = f32[3,8,16,16,8]{2,4,3,1,0:T(8,128)S(1)} copy(f32[3,8,16,16,8]{3,4,2,1,0:T(8,128)} %multiply_bitcast_fusion.1) | data formatting | bytes 393216 | tf_op jit(solution)/shard_map/transpose | solution.py:141
  78.2 1.5 collective-permute-start.9
  82.6 3.1 %collective-permute-done.9 = f32[3,8,16,16]{3,2,1,0:T(8,128)S(1)} collective-permute-done((f32[3,8,16,16]{3,2,1,0:T(8,128)S(1)}, f32[3,8,16,16]{3,2,1,0:T(8,128)S(1)}, u32[]{:S(2)}, u32[]{:S(2)}) %collective-permute-start.9) | collective-permute-done | bytes 24608 | tf_op jit(solution)/shard_map/ppermute | solution.py:27
  86.8 5.7 %collective-permute-start.10 = (f32[2,8,1,160]{3,2,1,0:T(1,128)S(1)}, f32[2,8,1,160]{3,2,1,0:T(1,128)S(1)}, u32[]{:S(2)}, u32[]{:S(2)}) collective-permute-start(f32[2,8,1,160]{3,2,1,0:T(1,128)S(1)} %get-tuple-element.85), channel_id=1, source_target_pairs={{0,1},{1,2},{2,3},{3,0},{4,5},{5,6},{6,7},{7,4},{8,9},{9,10},{10,1... | collective-permute-start | bytes 30728 | tf_op jit(solution)/shard_map/ppermute | solution.py:25
  93.4 2.3 %collective-permute-done.11 = f32[2,8,1,160]{3,2,1,0:T(1,128)S(1)} collective-permute-done((f32[2,8,1,160]{3,2,1,0:T(1,128)S(1)}, f32[2,8,1,160]{3,2,1,0:T(1,128)S(1)}, u32[]{:S(2)}, u32[]{:S(2)}) %collective-permute-start.11) | collective-permute-done | bytes 10272 | tf_op jit(solution)/shard_map/ppermute | solution.py:27
  98.6 1.9 collective-permute-done.13
  103.5 1.9 collective-permute-done.15
  106.4 3.5 %collective-permute-start.16 = (f32[7,8,16,16]{3,2,1,0:T(8,128)S(1)}, f32[7,8,16,16]{3,2,1,0:T(8,128)S(1)}, u32[]{:S(2)}, u32[]{:S(2)}) collective-permute-start(f32[7,8,16,16]{3,2,1,0:T(8,128)S(1)} %get-tuple-element.66), channel_id=1, source_target_pairs={{0,4},{4,8},{8,12},{12,16},{16,20},{20,24},{24,28},{1,5},{5,9},{9,... | collective-permute-start | bytes 172040 | tf_op jit(solution)/shard_map/ppermute | solution.py:25
  109.9 1.5 collective-permute-start.17
  112.7 7.5 %collective-permute-done.16 = f32[7,8,16,16]{3,2,1,0:T(8,128)S(1)} collective-permute-done((f32[7,8,16,16]{3,2,1,0:T(8,128)S(1)}, f32[7,8,16,16]{3,2,1,0:T(8,128)S(1)}, u32[]{:S(2)}, u32[]{:S(2)}) %collective-permute-start.16) | collective-permute-done | bytes 57376 | tf_op jit(solution)/shard_map/ppermute | solution.py:25
  120.2 11.9 %collective-permute-done.17 = f32[7,8,16,16]{3,2,1,0:T(8,128)S(1)} collective-permute-done((f32[7,8,16,16]{3,2,1,0:T(8,128)S(1)}, f32[7,8,16,16]{3,2,1,0:T(8,128)S(1)}, u32[]{:S(2)}, u32[]{:S(2)}) %collective-permute-start.17) | collective-permute-done | bytes 57376 | tf_op jit(solution)/shard_map/ppermute | solution.py:27
  134.4 1.7 subtract_convert_fusion.2
  137.7 11.8 %all_gather.7 = bf16[64,3072]{1,0:T(8,128)(2,1)S(1)} all-gather(bf16[16,3072]{1,0:T(8,128)(2,1)S(1)} %copy.68), channel_id=1, replica_groups=mesh['sec'=2,'gx'=4,'az'=4] {'gx'}, dimensions={0}, use_global_device_ids=true | all-gather | bytes 491520 | tf_op jit(solution)/shard_map/all_gather | solution.py:130
  153.1 4.4 %collective-permute-start.20 = (f32[2,8,1,160]{3,2,1,0:T(1,128)}, f32[2,8,1,160]{3,2,1,0:T(1,128)}, u32[]{:S(2)}, u32[]{:S(2)}) collective-permute-start(f32[2,8,1,160]{3,2,1,0:T(1,128)} %get-tuple-element.79), channel_id=1, source_target_pairs={{0,1},{1,2},{2,3},{3,0},{4,5},{5,6},{6,7},{7,4},{8,9},{9,10},{10,1... | collective-permute-start | bytes 30728 | tf_op jit(solution)/shard_map/ppermute | solution.py:25
  162.1 2.9 %multiply_bitcast_fusion = f32[3,8,16,16,8]{3,4,2,1,0:T(8,128)} fusion(f32[16,3,8,16,8]{0,4,3,2,1:T(8,128)} %bitcast.177, f32[16,3,8,16,8]{0,4,3,2,1:T(8,128)S(1)} %bitcast.176, f32[16]{0:T(128)S(1)} %copy-done.34, f32[16]{0:T(128)S(1)} %copy-done.33), kind=kLoop, calls=%fused_computation.6 | loop fusion | flops 196608 | bytes 589952 | tf_op jit(solution)/shard_map/transpose | solution.py:141
  165.0 2.0 %copy.71 = f32[3,8,16,16,8]{2,4,3,1,0:T(8,128)S(1)} copy(f32[3,8,16,16,8]{3,4,2,1,0:T(8,128)} %multiply_bitcast_fusion) | data formatting | bytes 393216 | tf_op jit(solution)/shard_map/transpose | solution.py:141
  168.9 1.8 fusion.127
  170.8 1.4 collective-permute-start.23
  173.5 4.4 %collective-permute-done.23 = f32[3,8,16,16]{3,2,1,0:T(8,128)S(1)} collective-permute-done((f32[3,8,16,16]{3,2,1,0:T(8,128)S(1)}, f32[3,8,16,16]{3,2,1,0:T(8,128)S(1)}, u32[]{:S(2)}, u32[]{:S(2)}) %collective-permute-start.23) | collective-permute-done | bytes 24608 | tf_op jit(solution)/shard_map/ppermute | solution.py:27
  179.1 3.1 %collective-permute-start.24 = (f32[2,8,1,160]{3,2,1,0:T(1,128)S(1)}, f32[2,8,1,160]{3,2,1,0:T(1,128)S(1)}, u32[]{:S(2)}, u32[]{:S(2)}) collective-permute-start(f32[2,8,1,160]{3,2,1,0:T(1,128)S(1)} %get-tuple-element.77), channel_id=1, source_target_pairs={{0,1},{1,2},{2,3},{3,0},{4,5},{5,6},{6,7},{7,4},{8,9},{9,10},{10,1... | collective-permute-start | bytes 30728 | tf_op jit(solution)/shard_map/ppermute | solution.py:25
  183.1 2.3 %collective-permute-done.25 = f32[2,8,1,160]{3,2,1,0:T(1,128)S(1)} collective-permute-done((f32[2,8,1,160]{3,2,1,0:T(1,128)S(1)}, f32[2,8,1,160]{3,2,1,0:T(1,128)S(1)}, u32[]{:S(2)}, u32[]{:S(2)}) %collective-permute-start.25) | collective-permute-done | bytes 10272 | tf_op jit(solution)/shard_map/ppermute | solution.py:27
  188.3 2.1 %collective-permute-done.27 = f32[2,8,1,160]{3,2,1,0:T(1,128)S(1)} collective-permute-done((f32[2,8,1,160]{3,2,1,0:T(1,128)S(1)}, f32[2,8,1,160]{3,2,1,0:T(1,128)S(1)}, u32[]{:S(2)}, u32[]{:S(2)}) %collective-permute-start.27) | collective-permute-done | bytes 10272 | tf_op jit(solution)/shard_map/ppermute | solution.py:27
  193.5 1.9 collective-permute-done.29
  (272 shorter events, 65.3 us)
Async XLA Ops:
  1.6 20.9 %collective-permute-start.2 = (f32[3,8,1,128]{3,2,1,0:T(1,128)S(1)}, f32[3,8,1,128]{3,2,1,0:T(1,128)S(1)}, u32[]{:S(2)}, u32[]{:S(2)}) collective-permute-start(f32[3,8,1,128]{3,2,1,0:T(1,128)S(1)} %get-tuple-element.108), channel_id=1, source_target_pairs={{0,1},{1,2},{2,3},{3,0},{4,5},{5,6},{6,7},{7,4},{8,9},{9,10},{10,1... | collective-permute-start | bytes 36872 | tf_op jit(solution)/shard_map/ppermute | solution.py:25
  4.3 19.5 %collective-permute-start.3 = (f32[3,8,1,128]{3,2,1,0:T(1,128)S(1)}, f32[3,8,1,128]{3,2,1,0:T(1,128)S(1)}, u32[]{:S(2)}, u32[]{:S(2)}) collective-permute-start(f32[3,8,1,128]{3,2,1,0:T(1,128)S(1)} %get-tuple-element.109), channel_id=1, source_target_pairs={{1,0},{2,1},{3,2},{0,3},{5,4},{6,5},{7,6},{4,7},{9,8},{10,9},{11,1... | collective-permute-start | bytes 36872 | tf_op jit(solution)/shard_map/ppermute | solution.py:27
  6.1 18.4 %collective-permute-start.4 = (f32[3,8,16,16]{3,2,1,0:T(8,128)}, f32[3,8,16,16]{3,2,1,0:T(8,128)}, u32[]{:S(2)}, u32[]{:S(2)}) collective-permute-start(f32[3,8,16,16]{3,2,1,0:T(8,128)} %get-tuple-element.97), channel_id=1, source_target_pairs={{0,4},{4,8},{8,12},{12,16},{16,20},{20,24},{24,28},{1,5},{5,9},{9,... | collective-permute-start | bytes 73736 | tf_op jit(solution)/shard_map/ppermute | solution.py:25
  10.1 14.4 %collective-permute-start.5 = (f32[3,8,16,16]{3,2,1,0:T(8,128)S(1)}, f32[3,8,16,16]{3,2,1,0:T(8,128)}, u32[]{:S(2)}, u32[]{:S(2)}) collective-permute-start(f32[3,8,16,16]{3,2,1,0:T(8,128)S(1)} %get-tuple-element.98), channel_id=1, source_target_pairs={{4,0},{8,4},{12,8},{16,12},{20,16},{24,20},{28,24},{5,1},{9,5},{13... | collective-permute-start | bytes 73736 | tf_op jit(solution)/shard_map/ppermute | solution.py:27
  14.4 12.9 %collective-permute-start = (f32[7,8,16,16]{3,2,1,0:T(8,128)}, f32[7,8,16,16]{3,2,1,0:T(8,128)S(1)}, u32[]{:S(2)}, u32[]{:S(2)}) collective-permute-start(f32[7,8,16,16]{3,2,1,0:T(8,128)} %get-tuple-element.68), channel_id=1, source_target_pairs={{0,4},{4,8},{8,12},{12,16},{16,20},{20,24},{24,28},{1,5},{5,9},{9,... | collective-permute-start | bytes 172040 | tf_op jit(solution)/shard_map/ppermute | solution.py:25
  20.5 25.1 %copy-start.15 = (f32[8,16,128]{2,1,0:T(8,128)}, f32[8,16,128]{2,1,0:T(8,128)S(1)}, u32[]{:S(2)}) copy-start(f32[8,16,128]{2,1,0:T(8,128)S(1)} %get-tuple-element.105) | copy-start | bytes 196612
  22.5 21.7 %collective-permute-start.1 = (f32[7,8,16,16]{3,2,1,0:T(8,128)S(1)}, f32[7,8,16,16]{3,2,1,0:T(8,128)S(1)}, u32[]{:S(2)}, u32[]{:S(2)}) collective-permute-start(f32[7,8,16,16]{3,2,1,0:T(8,128)S(1)} %get-tuple-element.69), channel_id=1, source_target_pairs={{4,0},{8,4},{12,8},{16,12},{20,16},{24,20},{28,24},{5,1},{9,5},{13... | collective-permute-start | bytes 172040 | tf_op jit(solution)/shard_map/ppermute | solution.py:27
  48.7 29.5 %collective-permute-start.6 = (f32[2,8,1,160]{3,2,1,0:T(1,128)}, f32[2,8,1,160]{3,2,1,0:T(1,128)}, u32[]{:S(2)}, u32[]{:S(2)}) collective-permute-start(f32[2,8,1,160]{3,2,1,0:T(1,128)} %get-tuple-element.87), channel_id=1, source_target_pairs={{0,1},{1,2},{2,3},{3,0},{4,5},{5,6},{6,7},{7,4},{8,9},{9,10},{10,1... | collective-permute-start | bytes 30728 | tf_op jit(solution)/shard_map/ppermute | solution.py:25
  49.3 30.4 %collective-permute-start.7 = (f32[2,8,1,160]{3,2,1,0:T(1,128)}, f32[2,8,1,160]{3,2,1,0:T(1,128)}, u32[]{:S(2)}, u32[]{:S(2)}) collective-permute-start(f32[2,8,1,160]{3,2,1,0:T(1,128)} %get-tuple-element.88), channel_id=1, source_target_pairs={{1,0},{2,1},{3,2},{0,3},{5,4},{6,5},{7,6},{4,7},{9,8},{10,9},{11,1... | collective-permute-start | bytes 30728 | tf_op jit(solution)/shard_map/ppermute | solution.py:27
  50.8 30.1 %collective-permute-start.18 = (f32[3,8,1,128]{3,2,1,0:T(1,128)}, f32[3,8,1,128]{3,2,1,0:T(1,128)}, u32[]{:S(2)}, u32[]{:S(2)}) collective-permute-start(f32[3,8,1,128]{3,2,1,0:T(1,128)} %get-tuple-element.99), channel_id=1, source_target_pairs={{0,1},{1,2},{2,3},{3,0},{4,5},{5,6},{6,7},{7,4},{8,9},{9,10},{10,1... | collective-permute-start | bytes 36872 | tf_op jit(solution)/shard_map/ppermute | solution.py:25
  52.6 28.4 %collective-permute-start.19 = (f32[3,8,1,128]{3,2,1,0:T(1,128)}, f32[3,8,1,128]{3,2,1,0:T(1,128)}, u32[]{:S(2)}, u32[]{:S(2)}) collective-permute-start(f32[3,8,1,128]{3,2,1,0:T(1,128)} %get-tuple-element.100), channel_id=1, source_target_pairs={{1,0},{2,1},{3,2},{0,3},{5,4},{6,5},{7,6},{4,7},{9,8},{10,9},{11,1... | collective-permute-start | bytes 36872 | tf_op jit(solution)/shard_map/ppermute | solution.py:27
  76.1 6.5 %collective-permute-start.8 = (f32[3,8,16,16]{3,2,1,0:T(8,128)S(1)}, f32[3,8,16,16]{3,2,1,0:T(8,128)S(1)}, u32[]{:S(2)}, u32[]{:S(2)}) collective-permute-start(f32[3,8,16,16]{3,2,1,0:T(8,128)S(1)} %get-tuple-element.94), channel_id=1, source_target_pairs={{0,4},{4,8},{8,12},{12,16},{16,20},{20,24},{24,28},{1,5},{5,9},{9,... | collective-permute-start | bytes 73736 | tf_op jit(solution)/shard_map/ppermute | solution.py:25
  78.2 7.4 %collective-permute-start.9 = (f32[3,8,16,16]{3,2,1,0:T(8,128)S(1)}, f32[3,8,16,16]{3,2,1,0:T(8,128)S(1)}, u32[]{:S(2)}, u32[]{:S(2)}) collective-permute-start(f32[3,8,16,16]{3,2,1,0:T(8,128)S(1)} %get-tuple-element.95), channel_id=1, source_target_pairs={{4,0},{8,4},{12,8},{16,12},{20,16},{24,20},{28,24},{5,1},{9,5},{13... | collective-permute-start | bytes 73736 | tf_op jit(solution)/shard_map/ppermute | solution.py:27
  86.8 6.6 %collective-permute-start.10 = (f32[2,8,1,160]{3,2,1,0:T(1,128)S(1)}, f32[2,8,1,160]{3,2,1,0:T(1,128)S(1)}, u32[]{:S(2)}, u32[]{:S(2)}) collective-permute-start(f32[2,8,1,160]{3,2,1,0:T(1,128)S(1)} %get-tuple-element.85), channel_id=1, source_target_pairs={{0,1},{1,2},{2,3},{3,0},{4,5},{5,6},{6,7},{7,4},{8,9},{9,10},{10,1... | collective-permute-start | bytes 30728 | tf_op jit(solution)/shard_map/ppermute | solution.py:25
  92.5 3.2 %collective-permute-start.11 = (f32[2,8,1,160]{3,2,1,0:T(1,128)S(1)}, f32[2,8,1,160]{3,2,1,0:T(1,128)S(1)}, u32[]{:S(2)}, u32[]{:S(2)}) collective-permute-start(f32[2,8,1,160]{3,2,1,0:T(1,128)S(1)} %get-tuple-element.86), channel_id=1, source_target_pairs={{1,0},{2,1},{3,2},{0,3},{5,4},{6,5},{7,6},{4,7},{9,8},{10,9},{11,1... | collective-permute-start | bytes 30728 | tf_op jit(solution)/shard_map/ppermute | solution.py:27
  97.2 1.4 collective-permute-start.12
  97.3 3.2 %collective-permute-start.13 = (f32[2,8,1,160]{3,2,1,0:T(1,128)S(1)}, f32[2,8,1,160]{3,2,1,0:T(1,128)S(1)}, u32[]{:S(2)}, u32[]{:S(2)}) collective-permute-start(f32[2,8,1,160]{3,2,1,0:T(1,128)S(1)} %get-tuple-element.84), channel_id=1, source_target_pairs={{1,0},{2,1},{3,2},{0,3},{5,4},{6,5},{7,6},{4,7},{9,8},{10,9},{11,1... | collective-permute-start | bytes 30728 | tf_op jit(solution)/shard_map/ppermute | solution.py:27
  102.1 1.4 collective-permute-start.14
  102.1 3.2 %collective-permute-start.15 = (f32[2,8,1,160]{3,2,1,0:T(1,128)S(1)}, f32[2,8,1,160]{3,2,1,0:T(1,128)S(1)}, u32[]{:S(2)}, u32[]{:S(2)}) collective-permute-start(f32[2,8,1,160]{3,2,1,0:T(1,128)S(1)} %get-tuple-element.82), channel_id=1, source_target_pairs={{1,0},{2,1},{3,2},{0,3},{5,4},{6,5},{7,6},{4,7},{9,8},{10,9},{11,1... | collective-permute-start | bytes 30728 | tf_op jit(solution)/shard_map/ppermute | solution.py:27
  106.4 13.8 %collective-permute-start.16 = (f32[7,8,16,16]{3,2,1,0:T(8,128)S(1)}, f32[7,8,16,16]{3,2,1,0:T(8,128)S(1)}, u32[]{:S(2)}, u32[]{:S(2)}) collective-permute-start(f32[7,8,16,16]{3,2,1,0:T(8,128)S(1)} %get-tuple-element.66), channel_id=1, source_target_pairs={{0,4},{4,8},{8,12},{12,16},{16,20},{20,24},{24,28},{1,5},{5,9},{9,... | collective-permute-start | bytes 172040 | tf_op jit(solution)/shard_map/ppermute | solution.py:25
  109.9 22.2 %collective-permute-start.17 = (f32[7,8,16,16]{3,2,1,0:T(8,128)S(1)}, f32[7,8,16,16]{3,2,1,0:T(8,128)S(1)}, u32[]{:S(2)}, u32[]{:S(2)}) collective-permute-start(f32[7,8,16,16]{3,2,1,0:T(8,128)S(1)} %get-tuple-element.67), channel_id=1, source_target_pairs={{4,0},{8,4},{12,8},{16,12},{20,16},{24,20},{28,24},{5,1},{9,5},{13... | collective-permute-start | bytes 172040 | tf_op jit(solution)/shard_map/ppermute | solution.py:27
  112.7 21.6 %copy-start.14 = (f32[6,8,16,128]{3,2,1,0:T(8,128)}, f32[6,8,16,128]{3,2,1,0:T(8,128)S(1)}, u32[]{:S(2)}) copy-start(f32[6,8,16,128]{3,2,1,0:T(8,128)S(1)} %fusion.1) | copy-start | bytes 1179652
  153.1 19.2 %collective-permute-start.20 = (f32[2,8,1,160]{3,2,1,0:T(1,128)}, f32[2,8,1,160]{3,2,1,0:T(1,128)}, u32[]{:S(2)}, u32[]{:S(2)}) collective-permute-start(f32[2,8,1,160]{3,2,1,0:T(1,128)} %get-tuple-element.79), channel_id=1, source_target_pairs={{0,1},{1,2},{2,3},{3,0},{4,5},{5,6},{6,7},{7,4},{8,9},{9,10},{10,1... | collective-permute-start | bytes 30728 | tf_op jit(solution)/shard_map/ppermute | solution.py:25
  157.4 14.9 %collective-permute-start.21 = (f32[2,8,1,160]{3,2,1,0:T(1,128)S(1)}, f32[2,8,1,160]{3,2,1,0:T(1,128)}, u32[]{:S(2)}, u32[]{:S(2)}) collective-permute-start(f32[2,8,1,160]{3,2,1,0:T(1,128)S(1)} %get-tuple-element.80), channel_id=1, source_target_pairs={{1,0},{2,1},{3,2},{0,3},{5,4},{6,5},{7,6},{4,7},{9,8},{10,9},{11,1... | collective-permute-start | bytes 30728 | tf_op jit(solution)/shard_map/ppermute | solution.py:27
  167.5 6.0 %collective-permute-start.22 = (f32[3,8,16,16]{3,2,1,0:T(8,128)S(1)}, f32[3,8,16,16]{3,2,1,0:T(8,128)S(1)}, u32[]{:S(2)}, u32[]{:S(2)}) collective-permute-start(f32[3,8,16,16]{3,2,1,0:T(8,128)S(1)} %get-tuple-element.89), channel_id=1, source_target_pairs={{0,4},{4,8},{8,12},{12,16},{16,20},{20,24},{24,28},{1,5},{5,9},{9,... | collective-permute-start | bytes 73736 | tf_op jit(solution)/shard_map/ppermute | solution.py:25
  170.8 7.1 %collective-permute-start.23 = (f32[3,8,16,16]{3,2,1,0:T(8,128)S(1)}, f32[3,8,16,16]{3,2,1,0:T(8,128)S(1)}, u32[]{:S(2)}, u32[]{:S(2)}) collective-permute-start(f32[3,8,16,16]{3,2,1,0:T(8,128)S(1)} %get-tuple-element.90), channel_id=1, source_target_pairs={{4,0},{8,4},{12,8},{16,12},{20,16},{24,20},{28,24},{5,1},{9,5},{13... | collective-permute-start | bytes 73736 | tf_op jit(solution)/shard_map/ppermute | solution.py:27
  179.1 4.0 %collective-permute-start.24 = (f32[2,8,1,160]{3,2,1,0:T(1,128)S(1)}, f32[2,8,1,160]{3,2,1,0:T(1,128)S(1)}, u32[]{:S(2)}, u32[]{:S(2)}) collective-permute-start(f32[2,8,1,160]{3,2,1,0:T(1,128)S(1)} %get-tuple-element.77), channel_id=1, source_target_pairs={{0,1},{1,2},{2,3},{3,0},{4,5},{5,6},{6,7},{7,4},{8,9},{9,10},{10,1... | collective-permute-start | bytes 30728 | tf_op jit(solution)/shard_map/ppermute | solution.py:25
  182.2 3.2 %collective-permute-start.25 = (f32[2,8,1,160]{3,2,1,0:T(1,128)S(1)}, f32[2,8,1,160]{3,2,1,0:T(1,128)S(1)}, u32[]{:S(2)}, u32[]{:S(2)}) collective-permute-start(f32[2,8,1,160]{3,2,1,0:T(1,128)S(1)} %get-tuple-element.78), channel_id=1, source_target_pairs={{1,0},{2,1},{3,2},{0,3},{5,4},{6,5},{7,6},{4,7},{9,8},{10,9},{11,1... | collective-permute-start | bytes 30728 | tf_op jit(solution)/shard_map/ppermute | solution.py:27
  186.9 1.4 collective-permute-start.26
  187.0 3.5 %collective-permute-start.27 = (f32[2,8,1,160]{3,2,1,0:T(1,128)S(1)}, f32[2,8,1,160]{3,2,1,0:T(1,128)S(1)}, u32[]{:S(2)}, u32[]{:S(2)}) collective-permute-start(f32[2,8,1,160]{3,2,1,0:T(1,128)S(1)} %get-tuple-element.76), channel_id=1, source_target_pairs={{1,0},{2,1},{3,2},{0,3},{5,4},{6,5},{7,6},{4,7},{9,8},{10,9},{11,1... | collective-permute-start | bytes 30728 | tf_op jit(solution)/shard_map/ppermute | solution.py:27
  192.1 1.4 collective-permute-start.28
  192.1 3.2 %collective-permute-start.29 = (f32[2,8,1,160]{3,2,1,0:T(1,128)S(1)}, f32[2,8,1,160]{3,2,1,0:T(1,128)S(1)}, u32[]{:S(2)}, u32[]{:S(2)}) collective-permute-start(f32[2,8,1,160]{3,2,1,0:T(1,128)S(1)} %get-tuple-element.74), channel_id=1, source_target_pairs={{1,0},{2,1},{3,2},{0,3},{5,4},{6,5},{7,6},{4,7},{9,8},{10,9},{11,1... | collective-permute-start | bytes 30728 | tf_op jit(solution)/shard_map/ppermute | solution.py:27
  (39 other events, 154.8 us)
where the time goes:
time: 198 us; the launch traced here: 197 us
  waiting for transfers between devices  57 us (29%)
  starting transfers between devices  41.6 us (21%)
  local copies, waits for them, and re-layouts  27.7 us (14%)
  other arithmetic  23.7 us (12%)
  blocking collectives  23.2 us (12%)
  matrix products  21.4 us (11%)
  between operations  2.21 us (1%)
    ppermute x15, waiting for transfers between devices, with_halo(): lax.ppermute(head, axis, [((i + 1) % count, i) for i in range(ends)])  48.7 us
    ppermute x15, starting transfers between devices, with_halo(): lax.ppermute(tail, axis, [(i, (i + 1) % count) for i in range(ends)])  32.7 us
    all_gather x2, blocking collectives, couple(): gathered = lax.all_gather(packed, 'gx', axis=0, tiled=True)  23.2 us
    ppermute x15, starting transfers between devices, with_halo(): lax.ppermute(head, axis, [((i + 1) % count, i) for i in range(ends)])  8.92 us
    ppermute x15, waiting for transfers between devices, with_halo(): lax.ppermute(tail, axis, [(i, (i + 1) % count) for i in range(ends)])  8.32 us
    dot_general x10, matrix products, stream_apply(): jnp.einsum('cras,st->crat', extended, matrix, precision=lax.Precision.HIG...  7.28 us
    dot_general x10, matrix products, azimuth_apply(): jnp.einsum('cras,at->crts', extended, matrix, precision=lax.Precision.HIG...  7.07 us
    dot_general x10, matrix products, radial_apply(): jnp.einsum('cras,rt->ctas', extended, matrix, precision=lax.Precision.HIG...  7 us
  transfers between devices with their start and end apart: 30, of which 12 were waited for; matrix products, arithmetic and copies ran while one was open for 24% of the time, Pallas kernels for 0%

commit v1 on v0

v1 whole, which is shorter than its diff:
```python
import functools

import jax
import jax.numpy as jnp
import numpy as np
from jax import lax
from jax.experimental import pallas as pl
from jax.experimental.pallas import tpu as pltpu
from jax.sharding import PartitionSpec as P

LES_STEPS = 2
CAA_SUB = 4

les_step = 0.02
caa_step = 0.01
mach_number = 0.5
block_nodes = 8
MESH = pl.DeviceIdType.MESH
F32 = jnp.float32
BF16 = jnp.bfloat16


def slope_table():
    points = np.array([-1.0, -(0.2**0.5), 0.2**0.5, 1.0])
    identity = np.eye(4)
    differences = points[:, None] - points[None, :] + identity
    inverse_weights = 1.0 / np.prod(differences, axis=1)
    slope_matrix = inverse_weights[None, :] / inverse_weights[:, None] / differences
    slope_matrix = slope_matrix * (1.0 - identity)
    return slope_matrix - identity * slope_matrix.sum(axis=1)[:, None]


def line_matrix(length):
    slope_matrix = slope_table()
    result = np.zeros((length + 2, length))
    for element in range(length // 4):
        at = 4 * element
        result[1 + at : 5 + at, at : at + 4] += slope_matrix.T
        result[at + 1, at] += 3.0
        result[at, at] -= 3.0
        result[at + 5, at + 3] += 3.0
        result[at + 4, at + 3] -= 3.0
    return result[1:-1].T


def halves(matrix):
    high = matrix.astype(np.float32).astype(BF16)
    low = (matrix - high.astype(np.float64)).astype(np.float32).astype(BF16)
    return high, low


def tables(radial, sector, stream):
    rows = radial * sector
    high, low = halves(line_matrix(stream).T)
    stream_mat = np.concatenate([high, high, low], axis=0)
    high, low = halves(np.kron(np.eye(radial), line_matrix(sector)))
    azimuth_mat = np.concatenate([high, high, low], axis=1)
    high, low = halves(np.kron(line_matrix(radial), np.eye(sector)))
    radial_mat = np.concatenate([high, high, low], axis=1)
    ghost = np.zeros((rows, 2 * radial))
    for r in range(radial):
        ghost[r * sector, r] = -3.0
        ghost[r * sector + sector - 1, radial + r] = 3.0
    azimuth_ghost = np.concatenate([ghost, ghost], axis=1).astype(BF16)
    ghost = np.zeros((16, 6 * stream))
    for c in range(6):
        ghost[c, c * stream] = -3.0
        ghost[8 + c, c * stream + stream - 1] = 3.0
    stream_ghost = np.concatenate([ghost, ghost], axis=0).astype(BF16)
    pick = np.zeros((16, 4 * stream))
    for c in range(4):
        pick[c, c * stream] = 1.0
        pick[8 + c, c * stream + stream - 1] = 1.0
    caa_pick = np.concatenate([pick, pick], axis=1).astype(BF16)
    pick = np.zeros((16, 3 * stream))
    for c in range(6):
        pick[c, (c % 3) * stream] = 1.0
        pick[8 + c, (c % 3) * stream + stream - 1] = 1.0
    les_pick = np.concatenate([pick, pick], axis=1).astype(BF16)
    return stream_mat, azimuth_mat, radial_mat, azimuth_ghost, stream_ghost, caa_pick, les_pick


def split(value):
    high = value.astype(BF16)
    return high, (value - high.astype(F32)).astype(BF16)


def product(left, right):
    return jnp.dot(left, right, preferred_element_type=F32)


def right_apply(fields, matrix):
    high, low = split(jnp.concatenate(fields, axis=0))
    return product(jnp.concatenate([high, low, high], axis=1), matrix)


def left_apply(matrix, fields):
    high, low = split(jnp.concatenate(fields, axis=1))
    return product(matrix, jnp.concatenate([high, low, high], axis=0))


def pick_edges(pick, fields):
    high, low = split(jnp.concatenate(fields, axis=1))
    return lax.dot_general(
        pick, jnp.concatenate([high, low], axis=1), (((1,), (1,)), ((), ())), preferred_element_type=F32
    )


def stream_fix(rim, ghost):
    high, low = split(rim)
    both = jnp.concatenate([high.astype(F32), low.astype(F32)], axis=0)
    return product(both.T.astype(BF16), ghost)


def azimuth_fix(ghost, rim):
    high, low = split(rim)
    return product(ghost, jnp.concatenate([high, low], axis=0))


def kernel(
    sizes,
    les_in, les_metric, caa_in, caa_metric, refs, offsets, send_list,
    stream_mat, azimuth_mat, radial_mat, azimuth_ghost, stream_ghost, caa_pick, les_pick,
    les_out, caa_out,
    source, weights, chooser,
    les_az_send, les_az_recv, les_st_send, les_st_recv,
    caa_az_send, caa_az_recv, caa_st_send, caa_st_recv,
    lamb_send, lamb_recv,
    les_sems, caa_sems, lamb_send_sem, lamb_recv_sem,
):
    n_sec, n_gx, n_az, radial, sector, stream, cap = sizes
    rows = radial * sector
    sec, gx, az = lax.axis_index("sec"), lax.axis_index("gx"), lax.axis_index("az")
    slabs = n_sec * n_gx
    slab = sec * n_gx + gx
    up, down = lax.rem(slab + slabs - 1, slabs), lax.rem(slab + 1, slabs)
    up_id = {"sec": up // n_gx, "gx": lax.rem(up, n_gx), "az": az}
    down_id = {"sec": down // n_gx, "gx": lax.rem(down, n_gx), "az": az}
    below_id = {"sec": sec, "gx": gx, "az": lax.rem(az + n_az - 1, n_az)}
    above_id = {"sec": sec, "gx": gx, "az": lax.rem(az + 1, n_az)}
    partners = [lax.rem(gx + k, n_gx) for k in range(1, n_gx)]

    barrier = pltpu.get_barrier_semaphore()
    for device in [up_id, down_id, below_id, above_id] + [{"sec": sec, "gx": d, "az": az} for d in partners]:
        pl.semaphore_signal(barrier, inc=1, device_id=device, device_id_type=MESH)

    lane = lax.broadcasted_iota(jnp.int32, (rows, stream), 1)
    row = lax.broadcasted_iota(jnp.int32, (rows, stream), 0)
    slot_lanes = cap * block_nodes
    groups = stream // slot_lanes
    slot_of_lane = lax.rem(lane, slot_lanes) // block_nodes
    slot_of_row = lax.rem(row, slot_lanes) // block_nodes
    node_of_lane = lax.rem(lane, block_nodes)
    same_node = lax.rem(row, block_nodes) == node_of_lane
    one_lane = lane[0:1]
    block_of_lane = one_lane // block_nodes
    lead = jnp.zeros((1, stream), jnp.int32)
    trail = jnp.zeros((1, stream), jnp.int32)
    part = jnp.zeros((1, stream), jnp.int32)
    for j in range(stream // block_nodes):
        here = block_of_lane == j
        lead = jnp.where(here, refs[j, 0] * cap + refs[j, 1], lead)
        trail = jnp.where(here, refs[j, 2] * cap + refs[j, 3], trail)
        part = jnp.where(here, offsets[j], part)
    trail_weight = part.astype(F32) / 8.0
    lead_weight = 1.0 - trail_weight
    for d in range(n_gx):
        code = slot_of_row + d * cap
        weight = jnp.where(code == lead, lead_weight, 0.0) + jnp.where(code == trail, trail_weight, 0.0)
        weights[d * stream : (d + 1) * stream, :] = jnp.where(same_node, weight, 0.0).astype(BF16)
        taken = jnp.zeros((1, stream), jnp.int32)
        for c in range(cap):
            taken = jnp.where(slot_of_lane[0:1] == c, send_list[slab, d, c], taken)
        wanted = taken * block_nodes + node_of_lane[0:1]
        chooser[:, d * stream : (d + 1) * stream] = jnp.where(row == wanted, 1.0, 0.0).astype(BF16)

    def four(sems, k, az_send, az_recv, st_send, st_recv):
        def copy(src, dst, way, device):
            return pltpu.make_async_remote_copy(
                src_ref=src.at[k, way % 2], dst_ref=dst.at[k, way % 2],
                send_sem=sems.at[k, way, 0], recv_sem=sems.at[k, way, 1],
                device_id=device, device_id_type=MESH,
            )

        return [
            copy(az_send, az_recv, 0, above_id),
            copy(az_send, az_recv, 1, below_id),
            copy(st_send, st_recv, 2, down_id),
            copy(st_send, st_recv, 3, up_id),
        ]

    def les_copies(k):
        return four(les_sems, k, les_az_send, les_az_recv, les_st_send, les_st_recv)

    def caa_copies(k):
        return four(caa_sems, k, caa_az_send, caa_az_recv, caa_st_send, caa_st_recv)

    def lamb_copy(k, d):
        return pltpu.make_async_remote_copy(
            src_ref=lamb_send.at[k, d], dst_ref=lamb_recv.at[k, gx],
            send_sem=lamb_send_sem.at[k, d], recv_sem=lamb_recv_sem.at[k, gx],
            device_id={"sec": sec, "gx": d, "az": az}, device_id_type=MESH,
        )

    def lamb_arrival(k, d):
        return pltpu.make_async_remote_copy(
            src_ref=lamb_send.at[k, d], dst_ref=lamb_recv.at[k, d],
            send_sem=lamb_send_sem.at[k, d], recv_sem=lamb_recv_sem.at[k, d],
            device_id={"sec": sec, "gx": d, "az": az}, device_id_type=MESH,
        )

    def ghosts(recv, k):
        before = jnp.where(slab > 0, recv[k, 0], 0.0)
        after = jnp.where(slab < slabs - 1, recv[k, 1], 0.0)
        return before, after

    def pieces(value, count):
        return [value[:, i * stream : (i + 1) * stream] for i in range(count)]

    pl.semaphore_wait(barrier, 4 + len(partners))

    for k in range(LES_STEPS):
        u_ref = les_in if k == 0 else les_out
        for c in range(3):
            les_az_send[k, 0, c * radial : (c + 1) * radial] = u_ref[c, pl.ds(sector - 1, radial, stride=sector), :]
            les_az_send[k, 1, c * radial : (c + 1) * radial] = u_ref[c, pl.ds(0, radial, stride=sector), :]
        copies = les_copies(k)
        copies[0].start()
        copies[1].start()
        u = [u_ref[c] for c in range(3)]
        edges = pick_edges(les_pick[...], u)
        les_st_send[k, 0] = edges[8:16]
        les_st_send[k, 1] = edges[0:8]
        copies[2].start()
        copies[3].start()

        stacked = [u + [u[j] * u[i] for i in range(3)] for j in range(3)]
        along = right_apply(stacked[0], stream_mat[...])
        along = [along[i * rows : (i + 1) * rows] for i in range(6)]
        around = pieces(left_apply(azimuth_mat[...], stacked[1]), 6)
        across = pieces(left_apply(radial_mat[...], stacked[2]), 6)

        for copy in copies:
            copy.wait_recv()
        before, after = ghosts(les_st_recv, k)
        third = lax.broadcasted_iota(jnp.int32, before.shape, 0) >= 3
        before = before * jnp.where(third, before[0:1], 1.0)
        after = after * jnp.where(third, after[0:1], 1.0)
        fix = pieces(stream_fix(jnp.concatenate([before, after], axis=0), stream_ghost[...]), 6)
        along = [a + b for a, b in zip(along, fix)]
        rim = []
        for c in range(3):
            rim.append([les_az_recv[k, way, c * radial : (c + 1) * radial] for way in range(2)])
        rim = rim + [[rim[1][way] * rim[c][way] for way in range(2)] for c in range(3)]
        rim = jnp.concatenate([jnp.concatenate(pair, axis=0) for pair in rim], axis=1)
        fix = pieces(azimuth_fix(azimuth_ghost[...], rim), 6)
        around = [a + b for a, b in zip(around, fix)]
        slopes = [
            [les_metric[0] * along[i] for i in range(3)],
            [les_metric[1] * around[i] for i in range(3)],
            [les_metric[2] * across[i] for i in range(3)],
        ]
        first = slopes[1][2] - slopes[2][1]
        second = slopes[2][0] - slopes[0][2]
        third = slopes[0][1] - slopes[1][0]
        lamb = jnp.concatenate(
            [
                second * u[2] - third * u[1],
                third * u[0] - first * u[2],
                first * u[1] - second * u[0],
            ],
            axis=0,
        ).astype(BF16)
        chosen = product(lamb, chooser[...])
        depth = 3 * rows // groups
        group_lane = lax.broadcasted_iota(jnp.int32, (depth, stream), 1) // slot_lanes
        for d in range(n_gx):
            mine = chosen[:, d * stream : (d + 1) * stream]
            packed = mine[0:depth]
            for g in range(1, groups):
                packed = jnp.where(group_lane == g, mine[g * depth : (g + 1) * depth], packed)
            lamb_send[k, d] = packed.astype(BF16)
        for d in partners:
            lamb_copy(k, d).start()
        lamb_recv[k, gx] = lamb_send[k, gx]

        for i in range(3):
            change = les_metric[0] * along[3 + i] + u[0] * slopes[0][i]
            change += les_metric[1] * around[3 + i] + u[1] * slopes[1][i]
            change += les_metric[2] * across[3 + i] + u[2] * slopes[2][i]
            les_out[i] = u[i] - (0.5 * les_step) * change

    for c in range(4):
        caa_out[c] = caa_in[c]

    def substep(k, carry):
        for way, at in ((0, sector - 1), (1, 0)):
            caa_az_send[k, way, 0:radial] = caa_out[0, pl.ds(at, radial, stride=sector), :]
            caa_az_send[k, way, radial : 2 * radial] = caa_out[2, pl.ds(at, radial, stride=sector), :]
        copies = caa_copies(k)
        copies[0].start()
        copies[1].start()
        w = [caa_out[c] for c in range(4)]
        edges = pick_edges(caa_pick[...], w)
        caa_st_send[k, 0] = edges[8:16]
        caa_st_send[k, 1] = edges[0:8]
        copies[2].start()
        copies[3].start()

        along = right_apply(w, stream_mat[...])
        along = [along[i * rows : (i + 1) * rows] for i in range(4)]
        around = pieces(left_apply(azimuth_mat[...], [w[0], w[2]]), 2)
        across = pieces(left_apply(radial_mat[...], [w[0], w[3]]), 2)

        for copy in copies:
            copy.wait_recv()
        fix = stream_fix(jnp.concatenate(ghosts(caa_st_recv, k), axis=0), stream_ghost[:, 0 : 4 * stream])
        along = [caa_metric[0] * (a + b) for a, b in zip(along, pieces(fix, 4))]
        rim = [
            jnp.concatenate([caa_az_recv[k, way, c * radial : (c + 1) * radial] for way in range(2)], axis=0)
            for c in range(2)
        ]
        fix = pieces(azimuth_fix(azimuth_ghost[...], jnp.concatenate(rim, axis=1)), 2)
        around = [caa_metric[1] * (a + b) for a, b in zip(around, fix)]
        across = [caa_metric[2] * a for a in across]
        rates = [
            mach_number * along[0] + along[1] + around[1] + across[1],
            mach_number * along[1] + along[0] - source[0:rows],
            mach_number * along[2] + around[0] - source[rows : 2 * rows],
            mach_number * along[3] + across[0] - source[2 * rows : 3 * rows],
        ]
        for c in range(4):
            caa_out[c] = w[c] - caa_step * rates[c]
        return carry

    for k in range(LES_STEPS):
        for d in partners:
            lamb_arrival(k, d).wait_recv()
        depth = 3 * rows // groups
        group_lane = lax.broadcasted_iota(jnp.int32, (depth, stream), 1) // slot_lanes
        for g in range(groups):
            got = [
                jnp.where(group_lane == g, lamb_recv[k, d].astype(F32), 0.0).astype(BF16) for d in range(n_gx)
            ]
            source[g * depth : (g + 1) * depth, :] = product(jnp.concatenate(got, axis=1), weights[...])
        lax.fori_loop(k * CAA_SUB, (k + 1) * CAA_SUB, substep, 0)

    def drain_caa(k, carry):
        for copy in caa_copies(k):
            copy.wait_send()
        return carry

    lax.fori_loop(0, LES_STEPS * CAA_SUB, drain_caa, 0)
    for k in range(LES_STEPS):
        for copy in les_copies(k):
            copy.wait_send()
        for d in partners:
            lamb_copy(k, d).wait_send()


def solution(mesh):
    n_sec, n_gx, n_az = mesh.shape["sec"], mesh.shape["gx"], mesh.shape["az"]

    def body(les_velocity, les_metric, caa_state, caa_metric, intersection_refs, offsets, send_list):
        radial, sector, stream = les_velocity.shape[1:]
        cap = send_list.shape[2]
        rows = radial * sector
        sizes = (n_sec, n_gx, n_az, radial, sector, stream, cap)
        consts = [jnp.asarray(t) for t in tables(radial, sector, stream)]
        flat = lambda x: x.reshape(x.shape[0], rows, stream)
        substeps = LES_STEPS * CAA_SUB
        depth = 3 * rows // (stream // (cap * block_nodes))
        vmem = pl.BlockSpec(memory_space=pltpu.VMEM)
        smem = pl.BlockSpec(memory_space=pltpu.SMEM)
        les_out, caa_out = pl.pallas_call(
            functools.partial(kernel, sizes),
            out_shape=(
                jax.ShapeDtypeStruct((3, rows, stream), F32),
                jax.ShapeDtypeStruct((4, rows, stream), F32),
            ),
            in_specs=[vmem] * 4 + [smem] * 3 + [vmem] * len(consts),
            out_specs=(vmem, vmem),
            scratch_shapes=[
                pltpu.VMEM((3 * rows, stream), F32),
                pltpu.VMEM((n_gx * stream, stream), BF16),
                pltpu.VMEM((rows, n_gx * stream), BF16),
                pltpu.VMEM((LES_STEPS, 2, 3 * radial, stream), F32),
                pltpu.VMEM((LES_STEPS, 2, 3 * radial, stream), F32),
                pltpu.VMEM((LES_STEPS, 2, 8, rows), F32),
                pltpu.VMEM((LES_STEPS, 2, 8, rows), F32),
                pltpu.VMEM((substeps, 2, 2 * radial, stream), F32),
                pltpu.VMEM((substeps, 2, 2 * radial, stream), F32),
                pltpu.VMEM((substeps, 2, 8, rows), F32),
                pltpu.VMEM((substeps, 2, 8, rows), F32),
                pltpu.VMEM((LES_STEPS, n_gx, depth, stream), BF16),
                pltpu.VMEM((LES_STEPS, n_gx, depth, stream), BF16),
                pltpu.SemaphoreType.DMA((LES_STEPS, 4, 2)),
                pltpu.SemaphoreType.DMA((substeps, 4, 2)),
                pltpu.SemaphoreType.DMA((LES_STEPS, n_gx)),
                pltpu.SemaphoreType.DMA((LES_STEPS, n_gx)),
            ],
            compiler_params=pltpu.CompilerParams(
                collective_id=0, has_side_effects=True, vmem_limit_bytes=40 * 2**20
            ),
        )(
            flat(les_velocity), flat(les_metric), flat(caa_state), flat(caa_metric),
            intersection_refs, offsets, send_list, *consts,
        )
        return les_out.reshape(les_velocity.shape), caa_out.reshape(caa_state.shape)

    in_specs = (
        P(None, None, "az", ("sec", "gx")),
        P(None, None, "az", ("sec", "gx")),
        P(None, None, "az", ("sec", "gx")),
        P(None, None, "az", ("sec", "gx")),
        P(("sec", "gx"), None),
        P(("sec", "gx")),
        P(),
    )
    out_specs = (P(None, None, "az", ("sec", "gx")), P(None, None, "az", ("sec", "gx")))
    return jax.shard_map(body, mesh=mesh, in_specs=in_specs, out_specs=out_specs, check_vma=False)
```

time: 198 us -> 69.5 us (0.35)
  the two profiles are of different devices: /device:TPU:1 before, /device:TPU:0 now
where the time goes in v1:
time: 69.5 us; the launch traced here: 68.9 us
  Pallas kernels  56.6 us (81%)
  local copies, waits for them, and re-layouts  11.6 us (17%)
    pallas_call x1, Pallas kernels, body(): pl.pallas_call(functools.partial(kernel, sizes), out_shape=(jax.ShapeDtyp...  56.6 us
    unnamed x29, local copies, waits for them, and re-layouts  11.6 us

profile of v1, /device:TPU:0, one launch (start us, length us, event | category | flops | bytes accessed | tf_op | source)
XLA Modules:
  0.0 68.9 jit_solution(9207272251928085341)
XLA Ops:
  0.6 0.0 copy-start.10
  0.6 0.0 copy-start.12
  0.7 0.8 %copy.16.refs = s32[16,4]{1,0:T(8,128)S(1)} copy(s32[16,4]{0,1:T(4,128)} %param.18) | data formatting | bytes 512 | tf_op args[4]
  1.4 0.0 copy-done.10
  1.4 0.0 copy-done.12
  1.4 0.0 copy-start
  1.4 0.9 %copy-done = f32[4,8,16,128]{3,2,1,0:T(8,128)S(1)} copy-done((f32[4,8,16,128]{3,2,1,0:T(8,128)S(1)}, f32[4,8,16,128]{3,2,1,0:T(8,128)}, u32[]{:S(2)}) %copy-start) | copy-done | bytes 262168
  2.4 0.0 copy-start.1
  2.4 0.9 %copy-done.1 = f32[3,8,16,128]{3,2,1,0:T(8,128)S(1)} copy-done((f32[3,8,16,128]{3,2,1,0:T(8,128)S(1)}, f32[3,8,16,128]{3,2,1,0:T(8,128)}, u32[]{:S(2)}) %copy-start.1) | copy-done | bytes 196632
  3.3 0.0 copy-start.2
  3.3 0.9 %copy-done.2 = f32[3,8,16,128]{3,2,1,0:T(8,128)S(1)} copy-done((f32[3,8,16,128]{3,2,1,0:T(8,128)S(1)}, f32[3,8,16,128]{3,2,1,0:T(8,128)}, u32[]{:S(2)}) %copy-start.2) | copy-done | bytes 196632
  4.2 0.0 copy-start.3
  4.2 0.9 %copy-done.3 = f32[3,8,16,128]{3,2,1,0:T(8,128)S(1)} copy-done((f32[3,8,16,128]{3,2,1,0:T(8,128)S(1)}, f32[3,8,16,128]{3,2,1,0:T(8,128)}, u32[]{:S(2)}) %copy-start.3) | copy-done | bytes 196632
  5.2 0.0 copy-start.4
  5.2 0.9 %copy-done.4 = bf16[128,384]{1,0:T(8,128)(2,1)S(1)} copy-done((bf16[128,384]{1,0:T(8,128)(2,1)S(1)}, bf16[128,384]{1,0:T(8,128)(2,1)}, u32[]{:S(2)}) %copy-start.4) | copy-done | bytes 98328
  6.1 0.0 copy-start.5
  6.1 0.9 %copy-done.5 = bf16[128,384]{1,0:T(8,128)(2,1)S(1)} copy-done((bf16[128,384]{1,0:T(8,128)(2,1)S(1)}, bf16[128,384]{1,0:T(8,128)(2,1)}, u32[]{:S(2)}) %copy-start.5) | copy-done | bytes 98328
  6.9 0.0 copy-start.6
  7.0 0.9 %copy-done.6 = bf16[384,128]{1,0:T(8,128)(2,1)S(1)} copy-done((bf16[384,128]{1,0:T(8,128)(2,1)S(1)}, bf16[384,128]{1,0:T(8,128)(2,1)}, u32[]{:S(2)}) %copy-start.6) | copy-done | bytes 98328
  7.8 0.0 copy-start.7
  7.8 0.8 %copy-done.7 = bf16[32,768]{1,0:T(8,128)(2,1)S(1)} copy-done((bf16[32,768]{1,0:T(8,128)(2,1)S(1)}, bf16[32,768]{1,0:T(8,128)(2,1)}, u32[]{:S(2)}) %copy-start.7) | copy-done | bytes 49176
  8.6 0.0 copy-start.8
  8.6 0.8 %copy-done.8 = bf16[16,1024]{1,0:T(8,128)(2,1)S(1)} copy-done((bf16[16,1024]{1,0:T(8,128)(2,1)S(1)}, bf16[16,1024]{1,0:T(8,128)(2,1)}, u32[]{:S(2)}) %copy-start.8) | copy-done | bytes 32792
  9.4 0.0 copy-start.9
  9.4 0.8 %copy-done.9 = bf16[128,32]{1,0:T(8,128)(2,1)S(1)} copy-done((bf16[128,32]{1,0:T(8,128)(2,1)S(1)}, bf16[128,32]{1,0:T(8,128)(2,1)}, u32[]{:S(2)}) %copy-start.9) | copy-done | bytes 8216
  10.2 0.0 copy-start.11
  10.2 0.7 %copy-done.11 = s32[8,4,8]{2,1,0:T(4,128)S(1)} copy-done((s32[8,4,8]{2,1,0:T(4,128)S(1)}, s32[8,4,8]{2,1,0:T(4,128)}, u32[]{:S(2)}) %copy-start.11) | copy-done | bytes 1048
  10.9 56.6 %shard_map.149 = (f32[3,128,128]{2,1,0:T(8,128)S(1)}, f32[4,128,128]{2,1,0:T(8,128)S(1)}) custom-call(f32[3,128,128]{2,1,0:T(8,128)S(1)} %bitcast.8, f32[3,128,128]{2,1,0:T(8,128)S(1)} %bitcast.9, f32[4,128,128]{2,1,0:T(8,128)S(1)} %bitcast.6, f32[3,128,128]{2,1,0:T(8,128)S(1)} %bitcast.10, s32[16,4]{1,0:T(8,128)S(1)} %copy.16.refs, s32[16]{0:T(128)S(1)} %copy-done.12, ...), custom_call_target="tpu_custom_call" | custom-call | tf_op jit(solution)/shard_map/pallas_call | solution.py:375
  67.5 0.7 copy.19
  68.2 0.7 %copy.20 = f32[4,8,16,128]{3,2,1,0:T(8,128)} copy(f32[4,8,16,128]{3,2,1,0:T(8,128)S(1)} %bitcast.7) | data formatting | bytes 524288
Async XLA Ops:
  0.6 0.8 %copy-start.10 = (bf16[16,768]{1,0:T(8,128)(2,1)S(1)}, bf16[16,768]{1,0:T(8,128)(2,1)}, u32[]{:S(2)}) copy-start(bf16[16,768]{1,0:T(8,128)(2,1)} %constant.20.clone.les_pick) | copy-start | bytes 73732
  0.6 0.8 %copy-start.12 = (s32[16]{0:T(128)S(1)}, s32[16]{0:T(128)}, u32[]{:S(2)}) copy-start(s32[16]{0:T(128)} %offsets.1) | copy-start | bytes 196
  1.4 1.0 %copy-start = (f32[4,8,16,128]{3,2,1,0:T(8,128)S(1)}, f32[4,8,16,128]{3,2,1,0:T(8,128)}, u32[]{:S(2)}) copy-start(f32[4,8,16,128]{3,2,1,0:T(8,128)} %param.16) | copy-start | bytes 786436
  2.4 0.9 %copy-start.1 = (f32[3,8,16,128]{3,2,1,0:T(8,128)S(1)}, f32[3,8,16,128]{3,2,1,0:T(8,128)}, u32[]{:S(2)}) copy-start(f32[3,8,16,128]{3,2,1,0:T(8,128)} %param.14) | copy-start | bytes 589828
  3.3 0.9 %copy-start.2 = (f32[3,8,16,128]{3,2,1,0:T(8,128)S(1)}, f32[3,8,16,128]{3,2,1,0:T(8,128)}, u32[]{:S(2)}) copy-start(f32[3,8,16,128]{3,2,1,0:T(8,128)} %param.15) | copy-start | bytes 589828
  4.2 0.9 %copy-start.3 = (f32[3,8,16,128]{3,2,1,0:T(8,128)S(1)}, f32[3,8,16,128]{3,2,1,0:T(8,128)}, u32[]{:S(2)}) copy-start(f32[3,8,16,128]{3,2,1,0:T(8,128)} %param.17) | copy-start | bytes 589828
  5.2 0.9 %copy-start.4 = (bf16[128,384]{1,0:T(8,128)(2,1)S(1)}, bf16[128,384]{1,0:T(8,128)(2,1)}, u32[]{:S(2)}) copy-start(bf16[128,384]{1,0:T(8,128)(2,1)} %constant.16.clone.radial_mat) | copy-start | bytes 294916
  6.1 0.9 %copy-start.5 = (bf16[128,384]{1,0:T(8,128)(2,1)S(1)}, bf16[128,384]{1,0:T(8,128)(2,1)}, u32[]{:S(2)}) copy-start(bf16[128,384]{1,0:T(8,128)(2,1)} %constant.15.clone.azimuth_mat) | copy-start | bytes 294916
  6.9 0.9 %copy-start.6 = (bf16[384,128]{1,0:T(8,128)(2,1)S(1)}, bf16[384,128]{1,0:T(8,128)(2,1)}, u32[]{:S(2)}) copy-start(bf16[384,128]{1,0:T(8,128)(2,1)} %constant.14.clone.stream_mat) | copy-start | bytes 294916
  7.8 0.8 %copy-start.7 = (bf16[32,768]{1,0:T(8,128)(2,1)S(1)}, bf16[32,768]{1,0:T(8,128)(2,1)}, u32[]{:S(2)}) copy-start(bf16[32,768]{1,0:T(8,128)(2,1)} %constant.18.clone.stream_ghost) | copy-start | bytes 147460
  8.6 0.8 %copy-start.8 = (bf16[16,1024]{1,0:T(8,128)(2,1)S(1)}, bf16[16,1024]{1,0:T(8,128)(2,1)}, u32[]{:S(2)}) copy-start(bf16[16,1024]{1,0:T(8,128)(2,1)} %constant.19.clone.caa_pick) | copy-start | bytes 98308
  9.4 0.8 %copy-start.9 = (bf16[128,32]{1,0:T(8,128)(2,1)S(1)}, bf16[128,32]{1,0:T(8,128)(2,1)}, u32[]{:S(2)}) copy-start(bf16[128,32]{1,0:T(8,128)(2,1)} %constant.17.clone.azimuth_ghost) | copy-start | bytes 24580
  10.2 0.7 %copy-start.11 = (s32[8,4,8]{2,1,0:T(4,128)S(1)}, s32[8,4,8]{2,1,0:T(4,128)}, u32[]{:S(2)}) copy-start(s32[8,4,8]{2,1,0:T(4,128)} %send_list.1) | copy-start | bytes 3076

commit v2 on v1

--- a/solution.py
+++ b/solution.py
@@ -77,7 +77,18 @@
         pick[c, (c % 3) * stream] = 1.0
         pick[8 + c, (c % 3) * stream + stream - 1] = 1.0
     les_pick = np.concatenate([pick, pick], axis=1).astype(BF16)
+    wide = [azimuth_mat, radial_mat, stream_ghost, caa_pick, les_pick]
+    azimuth_mat, radial_mat, stream_ghost, caa_pick, les_pick = [tall(t, stream) for t in wide]
     return stream_mat, azimuth_mat, radial_mat, azimuth_ghost, stream_ghost, caa_pick, les_pick
+
+
+def tall(table, width):
+    return np.concatenate([table[:, i : i + width] for i in range(0, table.shape[1], width)], axis=0)
+
+
+def wide(ref, height, count=None):
+    count = ref.shape[0] // height if count is None else count
+    return jnp.concatenate([ref[i * height : (i + 1) * height, :] for i in range(count)], axis=1)
 
 
 def split(value):
@@ -119,9 +130,12 @@
 
 def kernel(
     sizes,
-    les_in, les_metric, caa_in, caa_metric, refs, offsets, send_list,
+    les_hbm, les_metric_hbm, caa_hbm, caa_metric_hbm, refs_hbm, offsets_hbm, send_list_hbm,
+    stream_mat_hbm, azimuth_mat_hbm, radial_mat_hbm, azimuth_ghost_hbm, stream_ghost_hbm, caa_pick_hbm, les_pick_hbm,
+    les_out, caa_out,
+    les_in, les_metric, caa_metric, refs, offsets, send_list,
     stream_mat, azimuth_mat, radial_mat, azimuth_ghost, stream_ghost, caa_pick, les_pick,
-    les_out, caa_out,
+    load_sems,
     source, weights, chooser,
     les_az_send, les_az_recv, les_st_send, les_st_recv,
     caa_az_send, caa_az_recv, caa_st_send, caa_st_recv,
@@ -144,6 +158,24 @@
     for device in [up_id, down_id, below_id, above_id] + [{"sec": sec, "gx": d, "az": az} for d in partners]:
         pl.semaphore_signal(barrier, inc=1, device_id=device, device_id_type=MESH)
 
+    loads = [
+        pltpu.make_async_copy(src, dst, load_sems.at[i])
+        for i, (src, dst) in enumerate(
+            [
+                (refs_hbm, refs), (offsets_hbm, offsets), (send_list_hbm, send_list),
+                (les_hbm, les_in), (les_pick_hbm, les_pick),
+                (stream_mat_hbm, stream_mat), (azimuth_mat_hbm, azimuth_mat), (radial_mat_hbm, radial_mat),
+                (azimuth_ghost_hbm, azimuth_ghost), (stream_ghost_hbm, stream_ghost),
+                (les_metric_hbm, les_metric), (caa_hbm, caa_out), (caa_pick_hbm, caa_pick),
+                (caa_metric_hbm, caa_metric),
+            ]
+        )
+    ]
+    for load in loads:
+        load.start()
+    for load in loads[0:3]:
+        load.wait()
+
     lane = lax.broadcasted_iota(jnp.int32, (rows, stream), 1)
     row = lax.broadcasted_iota(jnp.int32, (rows, stream), 0)
     slot_lanes = cap * block_nodes
@@ -159,8 +191,8 @@
     part = jnp.zeros((1, stream), jnp.int32)
     for j in range(stream // block_nodes):
         here = block_of_lane == j
-        lead = jnp.where(here, refs[j, 0] * cap + refs[j, 1], lead)
-        trail = jnp.where(here, refs[j, 2] * cap + refs[j, 3], trail)
+        lead = jnp.where(here, refs[0, j] * cap + refs[1, j], lead)
+        trail = jnp.where(here, refs[2, j] * cap + refs[3, j], trail)
         part = jnp.where(here, offsets[j], part)
     trail_weight = part.astype(F32) / 8.0
     lead_weight = 1.0 - trail_weight
@@ -217,6 +249,8 @@
     def pieces(value, count):
         return [value[:, i * stream : (i + 1) * stream] for i in range(count)]
 
+    for load in loads[3:]:
+        load.wait()
     pl.semaphore_wait(barrier, 4 + len(partners))
 
     for k in range(LES_STEPS):
@@ -228,7 +262,7 @@
         copies[0].start()
         copies[1].start()
         u = [u_ref[c] for c in range(3)]
-        edges = pick_edges(les_pick[...], u)
+        edges = pick_edges(wide(les_pick, 16), u)
         les_st_send[k, 0] = edges[8:16]
         les_st_send[k, 1] = edges[0:8]
         copies[2].start()
@@ -237,8 +271,8 @@
         stacked = [u + [u[j] * u[i] for i in range(3)] for j in range(3)]
         along = right_apply(stacked[0], stream_mat[...])
         along = [along[i * rows : (i + 1) * rows] for i in range(6)]
-        around = pieces(left_apply(azimuth_mat[...], stacked[1]), 6)
-        across = pieces(left_apply(radial_mat[...], stacked[2]), 6)
+        around = pieces(left_apply(wide(azimuth_mat, rows), stacked[1]), 6)
+        across = pieces(left_apply(wide(radial_mat, rows), stacked[2]), 6)
 
         for copy in copies:
             copy.wait_recv()
@@ -246,7 +280,7 @@
         third = lax.broadcasted_iota(jnp.int32, before.shape, 0) >= 3
         before = before * jnp.where(third, before[0:1], 1.0)
         after = after * jnp.where(third, after[0:1], 1.0)
-        fix = pieces(stream_fix(jnp.concatenate([before, after], axis=0), stream_ghost[...]), 6)
+        fix = pieces(stream_fix(jnp.concatenate([before, after], axis=0), wide(stream_ghost, 32)), 6)
         along = [a + b for a, b in zip(along, fix)]
         rim = []
         for c in range(3):
@@ -290,9 +324,6 @@
             change += les_metric[2] * across[3 + i] + u[2] * slopes[2][i]
             les_out[i] = u[i] - (0.5 * les_step) * change
 
-    for c in range(4):
-        caa_out[c] = caa_in[c]
-
     def substep(k, carry):
         for way, at in ((0, sector - 1), (1, 0)):
             caa_az_send[k, way, 0:radial] = caa_out[0, pl.ds(at, radial, stride=sector), :]
@@ -301,7 +332,7 @@
         copies[0].start()
         copies[1].start()
         w = [caa_out[c] for c in range(4)]
-        edges = pick_edges(caa_pick[...], w)
+        edges = pick_edges(wide(caa_pick, 16), w)
         caa_st_send[k, 0] = edges[8:16]
         caa_st_send[k, 1] = edges[0:8]
         copies[2].start()
@@ -309,12 +340,12 @@
 
         along = right_apply(w, stream_mat[...])
         along = [along[i * rows : (i + 1) * rows] for i in range(4)]
-        around = pieces(left_apply(azimuth_mat[...], [w[0], w[2]]), 2)
-        across = pieces(left_apply(radial_mat[...], [w[0], w[3]]), 2)
+        around = pieces(left_apply(wide(azimuth_mat, rows), [w[0], w[2]]), 2)
+        across = pieces(left_apply(wide(radial_mat, rows), [w[0], w[3]]), 2)
 
         for copy in copies:
             copy.wait_recv()
-        fix = stream_fix(jnp.concatenate(ghosts(caa_st_recv, k), axis=0), stream_ghost[:, 0 : 4 * stream])
+        fix = stream_fix(jnp.concatenate(ghosts(caa_st_recv, k), axis=0), wide(stream_ghost, 32, 4))
         along = [caa_metric[0] * (a + b) for a, b in zip(along, pieces(fix, 4))]
         rim = [
             jnp.concatenate([caa_az_recv[k, way, c * radial : (c + 1) * radial] for way in range(2)], axis=0)
@@ -358,6 +389,17 @@
             lamb_copy(k, d).wait_send()
 
 
+def hand_over(les_from, caa_from, les_to, caa_to, sems):
+    copies = [
+        pltpu.make_async_copy(les_from, les_to, sems.at[0]),
+        pltpu.make_async_copy(caa_from, caa_to, sems.at[1]),
+    ]
+    for copy in copies:
+        copy.start()
+    for copy in copies:
+        copy.wait()
+
+
 def solution(mesh):
     n_sec, n_gx, n_az = mesh.shape["sec"], mesh.shape["gx"], mesh.shape["az"]
 
@@ -371,16 +413,26 @@
         substeps = LES_STEPS * CAA_SUB
         depth = 3 * rows // (stream // (cap * block_nodes))
         vmem = pl.BlockSpec(memory_space=pltpu.VMEM)
-        smem = pl.BlockSpec(memory_space=pltpu.SMEM)
+        hbm = pl.BlockSpec(memory_space=pltpu.HBM)
         les_out, caa_out = pl.pallas_call(
             functools.partial(kernel, sizes),
             out_shape=(
                 jax.ShapeDtypeStruct((3, rows, stream), F32),
                 jax.ShapeDtypeStruct((4, rows, stream), F32),
             ),
-            in_specs=[vmem] * 4 + [smem] * 3 + [vmem] * len(consts),
+            in_specs=[hbm] * (7 + len(consts)),
             out_specs=(vmem, vmem),
             scratch_shapes=[
+                pltpu.VMEM((3, rows, stream), F32),
+                pltpu.VMEM((3, rows, stream), F32),
+                pltpu.VMEM((3, rows, stream), F32),
+                pltpu.SMEM(intersection_refs.shape[::-1], jnp.int32),
+                pltpu.SMEM(offsets.shape, jnp.int32),
+                pltpu.SMEM(send_list.shape, jnp.int32),
+            ]
+            + [pltpu.VMEM(t.shape, BF16) for t in consts]
+            + [
+                pltpu.SemaphoreType.DMA((7 + len(consts),)),
                 pltpu.VMEM((3 * rows, stream), F32),
                 pltpu.VMEM((n_gx * stream, stream), BF16),
                 pltpu.VMEM((rows, n_gx * stream), BF16),
@@ -400,12 +452,23 @@
                 pltpu.SemaphoreType.DMA((LES_STEPS, n_gx)),
             ],
             compiler_params=pltpu.CompilerParams(
-                collective_id=0, has_side_effects=True, vmem_limit_bytes=40 * 2**20
+                collective_id=0, has_side_effects=True, vmem_limit_bytes=63 * 2**20
             ),
         )(
             flat(les_velocity), flat(les_metric), flat(caa_state), flat(caa_metric),
-            intersection_refs, offsets, send_list, *consts,
+            intersection_refs.T, offsets, send_list, *consts,
         )
+        les_out, caa_out = pl.pallas_call(
+            hand_over,
+            out_shape=(
+                jax.ShapeDtypeStruct((3, rows, stream), F32),
+                jax.ShapeDtypeStruct((4, rows, stream), F32),
+            ),
+            in_specs=[hbm] * 2,
+            out_specs=(hbm, hbm),
+            scratch_shapes=[pltpu.SemaphoreType.DMA((2,))],
+            compiler_params=pltpu.CompilerParams(vmem_limit_bytes=63 * 2**20),
+        )(les_out, caa_out)
         return les_out.reshape(les_velocity.shape), caa_out.reshape(caa_state.shape)
 
     in_specs = (

time: 69.5 us -> 72.4 us (1.042)
  Pallas kernels: 56.6 us -> 71.6 us
  local copies, waits for them, and re-layouts: 11.6 us -> 0 us
    pallas_call x0 -> x1, Pallas kernels: none -> 15 us  [body(): pl.pallas_call(hand_over, out_shape=(jax.ShapeDtypeStruct((3, rows, strea...]
    unnamed x29 -> x0, local copies, waits for them, and re-layouts: 11.6 us -> none
where the time goes in v2:
time: 72.4 us; the launch traced here: 72.2 us
  Pallas kernels  71.6 us (99%)
    pallas_call x1, Pallas kernels, body(): pl.pallas_call(functools.partial(kernel, sizes), out_shape=(jax.ShapeDtyp...  56.6 us
    pallas_call x1, Pallas kernels, body(): pl.pallas_call(hand_over, out_shape=(jax.ShapeDtypeStruct((3, rows, strea...  15 us

profile of v2, /device:TPU:0, one launch (start us, length us, event | category | flops | bytes accessed | tf_op | source)
XLA Modules:
  0.0 72.2 jit_solution(15424557084833292437)
XLA Ops:
  0.6 56.6 %shard_map.149 = (f32[3,128,128]{2,1,0:T(8,128)}, f32[4,128,128]{2,1,0:T(8,128)}) custom-call(f32[3,128,128]{2,1,0:T(8,128)} %bitcast.8, f32[3,128,128]{2,1,0:T(8,128)} %bitcast.9, f32[4,128,128]{2,1,0:T(8,128)} %bitcast.7, f32[3,128,128]{2,1,0:T(8,128)} %bitcast.10, s32[4,16]{1,0:T(4,128)} %bitcast.11, s32[16]{0:T(128)} %offsets_hbm.1, ...), custom_call_target="tpu_custom_call" | custom-call | tf_op jit(solution)/shard_map/pallas_call | solution.py:417
  57.2 15.0 %shard_map.150 = (f32[3,128,128]{2,1,0:T(8,128)}, f32[4,128,128]{2,1,0:T(8,128)}) custom-call(f32[3,128,128]{2,1,0:T(8,128)} %get-tuple-element.6.les_from, f32[4,128,128]{2,1,0:T(8,128)} %get-tuple-element.7.caa_from), custom_call_target="tpu_custom_call" | custom-call | tf_op jit(solution)/shard_map/pallas_call | solution.py:461

commit v3 on v2

--- a/solution.py
+++ b/solution.py
@@ -15,6 +15,7 @@
 caa_step = 0.01
 mach_number = 0.5
 block_nodes = 8
+margin_nodes = 16
 MESH = pl.DeviceIdType.MESH
 F32 = jnp.float32
 BF16 = jnp.bfloat16
@@ -67,19 +68,31 @@
         ghost[c, c * stream] = -3.0
         ghost[8 + c, c * stream + stream - 1] = 3.0
     stream_ghost = np.concatenate([ghost, ghost], axis=0).astype(BF16)
-    pick = np.zeros((16, 4 * stream))
-    for c in range(4):
-        pick[c, c * stream] = 1.0
-        pick[8 + c, c * stream + stream - 1] = 1.0
-    caa_pick = np.concatenate([pick, pick], axis=1).astype(BF16)
     pick = np.zeros((16, 3 * stream))
     for c in range(6):
         pick[c, (c % 3) * stream] = 1.0
         pick[8 + c, (c % 3) * stream + stream - 1] = 1.0
     les_pick = np.concatenate([pick, pick], axis=1).astype(BF16)
-    wide = [azimuth_mat, radial_mat, stream_ghost, caa_pick, les_pick]
-    azimuth_mat, radial_mat, stream_ghost, caa_pick, les_pick = [tall(t, stream) for t in wide]
-    return stream_mat, azimuth_mat, radial_mat, azimuth_ghost, stream_ghost, caa_pick, les_pick
+    m = margin_nodes
+    inner = np.zeros((stream, 4 * stream))
+    mix = mach_number * np.eye(4)
+    mix[1, 0] = mix[0, 1] = 1.0
+    joint = np.zeros((4, stream, stream))
+    spread = np.zeros((stream, 3 * stream))
+    for c in range(4):
+        inner[2 * m * c + m - 1, c * stream] = -3.0
+        inner[2 * m * c + m, c * stream + stream - 1] = 3.0
+        for o in range(4):
+            joint[c, 0, 2 * m * o + m - 1] = 3.0 * mix[c, o]
+            joint[c, stream - 1, 2 * m * o + m] = -3.0 * mix[c, o]
+            if c < 3:
+                for t in range(2 * m):
+                    spread[2 * m * c + t, c * stream + 2 * m * o + t] = 1.0
+    high, low = halves(np.kron(mix, np.kron(np.eye(2), line_matrix(m).T)))
+    joint = [joint[c // 2].astype(BF16) for c in range(8)]
+    margin_mat = np.concatenate([high, high, low] + joint, axis=0)
+    columns = [azimuth_mat, radial_mat, stream_ghost, les_pick, inner.astype(BF16), spread.astype(BF16)]
+    return [stream_mat, azimuth_ghost, margin_mat] + [tall(t, stream) for t in columns]
 
 
 def tall(table, width):
@@ -131,16 +144,17 @@
 def kernel(
     sizes,
     les_hbm, les_metric_hbm, caa_hbm, caa_metric_hbm, refs_hbm, offsets_hbm, send_list_hbm,
-    stream_mat_hbm, azimuth_mat_hbm, radial_mat_hbm, azimuth_ghost_hbm, stream_ghost_hbm, caa_pick_hbm, les_pick_hbm,
+    stream_mat_hbm, azimuth_ghost_hbm, margin_mat_hbm,
+    azimuth_mat_hbm, radial_mat_hbm, stream_ghost_hbm, les_pick_hbm, inner_hbm, spread_hbm,
     les_out, caa_out,
     les_in, les_metric, caa_metric, refs, offsets, send_list,
-    stream_mat, azimuth_mat, radial_mat, azimuth_ghost, stream_ghost, caa_pick, les_pick,
+    stream_mat, azimuth_ghost, margin_mat, azimuth_mat, radial_mat, stream_ghost, les_pick, inner, spread,
     load_sems,
     source, weights, chooser,
     les_az_send, les_az_recv, les_st_send, les_st_recv,
-    caa_az_send, caa_az_recv, caa_st_send, caa_st_recv,
+    caa_az_send, caa_az_recv, margin_send, margin_recv, margin, margin_metric, margin_source,
     lamb_send, lamb_recv,
-    les_sems, caa_sems, lamb_send_sem, lamb_recv_sem,
+    les_sems, caa_sems, margin_sems, lamb_send_sem, lamb_recv_sem,
 ):
     n_sec, n_gx, n_az, radial, sector, stream, cap = sizes
     rows = radial * sector
@@ -166,7 +180,7 @@
                 (les_hbm, les_in), (les_pick_hbm, les_pick),
                 (stream_mat_hbm, stream_mat), (azimuth_mat_hbm, azimuth_mat), (radial_mat_hbm, radial_mat),
                 (azimuth_ghost_hbm, azimuth_ghost), (stream_ghost_hbm, stream_ghost),
-                (les_metric_hbm, les_metric), (caa_hbm, caa_out), (caa_pick_hbm, caa_pick),
+                (les_metric_hbm, les_metric), (caa_hbm, caa_out), (margin_mat_hbm, margin_mat), (inner_hbm, inner), (spread_hbm, spread),
                 (caa_metric_hbm, caa_metric),
             ]
         )
@@ -206,26 +220,59 @@
         wanted = taken * block_nodes + node_of_lane[0:1]
         chooser[:, d * stream : (d + 1) * stream] = jnp.where(row == wanted, 1.0, 0.0).astype(BF16)
 
-    def four(sems, k, az_send, az_recv, st_send, st_recv):
-        def copy(src, dst, way, device):
-            return pltpu.make_async_remote_copy(
-                src_ref=src.at[k, way % 2], dst_ref=dst.at[k, way % 2],
-                send_sem=sems.at[k, way, 0], recv_sem=sems.at[k, way, 1],
-                device_id=device, device_id_type=MESH,
+    def pair(sems, k, first, send, recv, devices):
+        return [
+            pltpu.make_async_remote_copy(
+                src_ref=send.at[k, way], dst_ref=recv.at[k, way],
+                send_sem=sems.at[k, first + way, 0], recv_sem=sems.at[k, first + way, 1],
+                device_id=devices[way], device_id_type=MESH,
             )
-
+            for way in range(2)
+        ]
+
+    def les_copies(k):
+        copies = pair(les_sems, k, 0, les_az_send, les_az_recv, (above_id, below_id))
+        return copies + pair(les_sems, k, 2, les_st_send, les_st_recv, (down_id, up_id))
+
+    def caa_copies(k):
+        return pair(caa_sems, k, 0, caa_az_send, caa_az_recv, (above_id, below_id))
+
+    def margin_copies(i):
         return [
-            copy(az_send, az_recv, 0, above_id),
-            copy(az_send, az_recv, 1, below_id),
-            copy(st_send, st_recv, 2, down_id),
-            copy(st_send, st_recv, 3, up_id),
+            pltpu.make_async_remote_copy(
+                src_ref=margin_send.at[i], dst_ref=margin_recv.at[i, way],
+                send_sem=margin_sems.at[i, way, 0], recv_sem=margin_sems.at[i, way, 1],
+                device_id=(down_id, up_id)[way], device_id_type=MESH,
+            )
+            for way in range(2)
         ]
 
-    def les_copies(k):
-        return four(les_sems, k, les_az_send, les_az_recv, les_st_send, les_st_recv)
-
-    def caa_copies(k):
-        return four(caa_sems, k, caa_az_send, caa_az_recv, caa_st_send, caa_st_recv)
+    width = 2 * margin_nodes
+    group = lane // width
+
+    def send_margin(i, fields, first):
+        packed = jnp.zeros((rows, stream), F32)
+        for c, field in enumerate(fields, first):
+            packed = jnp.where(group == c, pltpu.roll(field, width * c + margin_nodes, 1), packed)
+        margin_send[i] = packed.astype(BF16)
+        for copy in margin_copies(i):
+            copy.start()
+
+    def take_margin(i):
+        for copy in margin_copies(i):
+            copy.wait_recv()
+        before = jnp.where(slab > 0, margin_recv[i, 0].astype(F32), 0.0)
+        after = jnp.where(slab < slabs - 1, margin_recv[i, 1].astype(F32), 0.0)
+        return jnp.where(lax.rem(lane, width) < margin_nodes, before, after)
+
+    def swap_azimuth(value):
+        at = lax.broadcasted_iota(jnp.int32, value.shape, 1) // width
+        return jnp.where(lax.rem(at, 2) == 0, pltpu.roll(value, 2 * width, 1), 0.0)
+
+    def swap_radial(value):
+        return jnp.where(
+            group == 0, pltpu.roll(value, width, 1), jnp.where(group == 3, pltpu.roll(value, 3 * width, 1), 0.0)
+        )
 
     def lamb_copy(k, d):
         return pltpu.make_async_remote_copy(
@@ -267,6 +314,9 @@
         les_st_send[k, 1] = edges[0:8]
         copies[2].start()
         copies[3].start()
+        if k == 0:
+            send_margin(0, [caa_metric[c] for c in range(3)], 0)
+            send_margin(1, [caa_out[c] for c in range(4)], 0)
 
         stacked = [u + [u[j] * u[i] for i in range(3)] for j in range(3)]
         along = right_apply(stacked[0], stream_mat[...])
@@ -324,47 +374,59 @@
             change += les_metric[2] * across[3 + i] + u[2] * slopes[2][i]
             les_out[i] = u[i] - (0.5 * les_step) * change
 
-    def substep(k, carry):
+    def substep(k, fresh):
+        w = [caa_out[c] for c in range(4)]
+        m = margin[...]
         for way, at in ((0, sector - 1), (1, 0)):
-            caa_az_send[k, way, 0:radial] = caa_out[0, pl.ds(at, radial, stride=sector), :]
-            caa_az_send[k, way, radial : 2 * radial] = caa_out[2, pl.ds(at, radial, stride=sector), :]
+            ring = pl.ds(at, radial, stride=sector)
+            caa_az_send[k, way, 0:radial] = caa_out[0, ring, :]
+            caa_az_send[k, way, radial : 2 * radial] = caa_out[2, ring, :]
+            caa_az_send[k, way, 2 * radial : 3 * radial] = swap_azimuth(margin[ring, :])
         copies = caa_copies(k)
-        copies[0].start()
-        copies[1].start()
-        w = [caa_out[c] for c in range(4)]
-        edges = pick_edges(wide(caa_pick, 16), w)
-        caa_st_send[k, 0] = edges[8:16]
-        caa_st_send[k, 1] = edges[0:8]
-        copies[2].start()
-        copies[3].start()
-
-        along = right_apply(w, stream_mat[...])
-        along = [along[i * rows : (i + 1) * rows] for i in range(4)]
-        around = pieces(left_apply(wide(azimuth_mat, rows), [w[0], w[2]]), 2)
-        across = pieces(left_apply(wide(radial_mat, rows), [w[0], w[3]]), 2)
+        for copy in copies:
+            copy.start()
+
+        high, low = split(jnp.concatenate(w, axis=0))
+        m_high, m_low = split(m)
+        along = product(jnp.concatenate([high, low, high], axis=1), stream_mat[...])
+        table = wide(inner, rows)
+        fix = product(jnp.concatenate([m_high, m_low], axis=1), jnp.concatenate([table, table], axis=0))
+        along = [caa_metric[0] * (along[i * rows : (i + 1) * rows] + b) for i, b in enumerate(pieces(fix, 4))]
+        parts = [m_high, m_low, m_high]
+        for c in range(4):
+            parts += [high[c * rows : (c + 1) * rows], low[c * rows : (c + 1) * rows]]
+        m_along = product(jnp.concatenate(parts, axis=1), margin_mat[...])
+        around = pieces(left_apply(wide(azimuth_mat, rows), [w[0], w[2], swap_azimuth(m)]), 3)
+        across = pieces(left_apply(wide(radial_mat, rows), [w[0], w[3], swap_radial(m)]), 3)
 
         for copy in copies:
             copy.wait_recv()
-        fix = stream_fix(jnp.concatenate(ghosts(caa_st_recv, k), axis=0), wide(stream_ghost, 32, 4))
-        along = [caa_metric[0] * (a + b) for a, b in zip(along, pieces(fix, 4))]
         rim = [
             jnp.concatenate([caa_az_recv[k, way, c * radial : (c + 1) * radial] for way in range(2)], axis=0)
-            for c in range(2)
+            for c in range(3)
         ]
-        fix = pieces(azimuth_fix(azimuth_ghost[...], jnp.concatenate(rim, axis=1)), 2)
-        around = [caa_metric[1] * (a + b) for a, b in zip(around, fix)]
-        across = [caa_metric[2] * a for a in across]
+        fix = pieces(azimuth_fix(azimuth_ghost[...], jnp.concatenate(rim, axis=1)), 3)
+        around = [a + b for a, b in zip(around, fix)]
         rates = [
-            mach_number * along[0] + along[1] + around[1] + across[1],
+            mach_number * along[0] + along[1] + caa_metric[1] * around[1] + caa_metric[2] * across[1],
             mach_number * along[1] + along[0] - source[0:rows],
-            mach_number * along[2] + around[0] - source[rows : 2 * rows],
-            mach_number * along[3] + across[0] - source[2 * rows : 3 * rows],
+            mach_number * along[2] + caa_metric[1] * around[0] - source[rows : 2 * rows],
+            mach_number * along[3] + caa_metric[2] * across[0] - source[2 * rows : 3 * rows],
         ]
         for c in range(4):
             caa_out[c] = w[c] - caa_step * rates[c]
+        if fresh is not None:
+            margin_source[...] = take_margin(fresh)
+        rate = margin_metric[0] * m_along + margin_metric[1] * around[2] + margin_metric[2] * across[2]
+        margin[...] = m - caa_step * (rate - margin_source[...])
+
+    def later_substep(k, carry):
+        substep(k, None)
         return carry
 
     for k in range(LES_STEPS):
+        if k > 0:
+            send_margin(1 + 2 * k, [caa_out[c] for c in range(4)], 0)
         for d in partners:
             lamb_arrival(k, d).wait_recv()
         depth = 3 * rows // groups
@@ -374,7 +436,15 @@
                 jnp.where(group_lane == g, lamb_recv[k, d].astype(F32), 0.0).astype(BF16) for d in range(n_gx)
             ]
             source[g * depth : (g + 1) * depth, :] = product(jnp.concatenate(got, axis=1), weights[...])
-        lax.fori_loop(k * CAA_SUB, (k + 1) * CAA_SUB, substep, 0)
+        send_margin(2 + 2 * k, [source[c * rows : (c + 1) * rows, :] for c in range(3)], 1)
+        if k == 0:
+            table = wide(spread, rows)
+            spread_metric = pieces(product(take_margin(0).astype(BF16), table), 3)
+            for c in range(3):
+                margin_metric[c] = spread_metric[c]
+        margin[...] = take_margin(1 + 2 * k)
+        substep(k * CAA_SUB, 2 + 2 * k)
+        lax.fori_loop(k * CAA_SUB + 1, (k + 1) * CAA_SUB, later_substep, 0)
 
     def drain_caa(k, carry):
         for copy in caa_copies(k):
@@ -382,6 +452,9 @@
         return carry
 
     lax.fori_loop(0, LES_STEPS * CAA_SUB, drain_caa, 0)
+    for i in range(1 + 2 * LES_STEPS):
+        for copy in margin_copies(i):
+            copy.wait_send()
     for k in range(LES_STEPS):
         for copy in les_copies(k):
             copy.wait_send()
@@ -389,15 +462,17 @@
             lamb_copy(k, d).wait_send()
 
 
-def hand_over(les_from, caa_from, les_to, caa_to, sems):
-    copies = [
-        pltpu.make_async_copy(les_from, les_to, sems.at[0]),
-        pltpu.make_async_copy(caa_from, caa_to, sems.at[1]),
-    ]
-    for copy in copies:
-        copy.start()
-    for copy in copies:
-        copy.wait()
+def hand_over(les_from, caa_from, les_to, caa_to, les_held, caa_held, sems):
+    chains = ((les_from, les_held, les_to), (caa_from, caa_held, caa_to))
+    loads = [pltpu.make_async_copy(a, b, sems.at[i]) for i, (a, b, _) in enumerate(chains)]
+    stores = [pltpu.make_async_copy(b, c, sems.at[2 + i]) for i, (_, b, c) in enumerate(chains)]
+    for load in loads:
+        load.start()
+    for load, store in zip(loads, stores):
+        load.wait()
+        store.start()
+    for store in stores:
+        store.wait()
 
 
 def solution(mesh):
@@ -440,14 +515,18 @@
                 pltpu.VMEM((LES_STEPS, 2, 3 * radial, stream), F32),
                 pltpu.VMEM((LES_STEPS, 2, 8, rows), F32),
                 pltpu.VMEM((LES_STEPS, 2, 8, rows), F32),
-                pltpu.VMEM((substeps, 2, 2 * radial, stream), F32),
-                pltpu.VMEM((substeps, 2, 2 * radial, stream), F32),
-                pltpu.VMEM((substeps, 2, 8, rows), F32),
-                pltpu.VMEM((substeps, 2, 8, rows), F32),
+                pltpu.VMEM((substeps, 2, 3 * radial, stream), F32),
+                pltpu.VMEM((substeps, 2, 3 * radial, stream), F32),
+                pltpu.VMEM((1 + 2 * LES_STEPS, rows, stream), BF16),
+                pltpu.VMEM((1 + 2 * LES_STEPS, 2, rows, stream), BF16),
+                pltpu.VMEM((rows, stream), F32),
+                pltpu.VMEM((3, rows, stream), F32),
+                pltpu.VMEM((rows, stream), F32),
                 pltpu.VMEM((LES_STEPS, n_gx, depth, stream), BF16),
                 pltpu.VMEM((LES_STEPS, n_gx, depth, stream), BF16),
                 pltpu.SemaphoreType.DMA((LES_STEPS, 4, 2)),
-                pltpu.SemaphoreType.DMA((substeps, 4, 2)),
+                pltpu.SemaphoreType.DMA((substeps, 2, 2)),
+                pltpu.SemaphoreType.DMA((1 + 2 * LES_STEPS, 2, 2)),
                 pltpu.SemaphoreType.DMA((LES_STEPS, n_gx)),
                 pltpu.SemaphoreType.DMA((LES_STEPS, n_gx)),
             ],
@@ -458,15 +537,13 @@
             flat(les_velocity), flat(les_metric), flat(caa_state), flat(caa_metric),
             intersection_refs.T, offsets, send_list, *consts,
         )
+        shapes = [(3, rows, stream), (4, rows, stream)]
         les_out, caa_out = pl.pallas_call(
             hand_over,
-            out_shape=(
-                jax.ShapeDtypeStruct((3, rows, stream), F32),
-                jax.ShapeDtypeStruct((4, rows, stream), F32),
-            ),
+            out_shape=tuple(jax.ShapeDtypeStruct(shape, F32) for shape in shapes),
             in_specs=[hbm] * 2,
             out_specs=(hbm, hbm),
-            scratch_shapes=[pltpu.SemaphoreType.DMA((2,))],
+            scratch_shapes=[pltpu.VMEM(shape, F32) for shape in shapes] + [pltpu.SemaphoreType.DMA((4,))],
             compiler_params=pltpu.CompilerParams(vmem_limit_bytes=63 * 2**20),
         )(les_out, caa_out)
         return les_out.reshape(les_velocity.shape), caa_out.reshape(caa_state.shape)

time: 72.4 us -> 49.3 us (0.68)
  the two profiles are of different devices: /device:TPU:0 before, /device:TPU:1 now
where the time goes in v3:
time: 49.3 us; the launch traced here: 49.1 us
  Pallas kernels  48.4 us (98%)
  between operations  0.64 us (1%)
    pallas_call x1, Pallas kernels, body(): pl.pallas_call(functools.partial(kernel, sizes), out_shape=(jax.ShapeDtyp...  46.6 us
    pallas_call x1, Pallas kernels, body(): pl.pallas_call(hand_over, out_shape=tuple((jax.ShapeDtypeStruct(shape, F3...  1.79 us

profile of v3, /device:TPU:1, one launch (start us, length us, event | category | flops | bytes accessed | tf_op | source)
XLA Modules:
  0.0 49.1 jit_solution(10720251889027384480)
XLA Ops:
  0.6 46.6 %shard_map.167 = (f32[3,128,128]{2,1,0:T(8,128)}, f32[4,128,128]{2,1,0:T(8,128)}) custom-call(f32[3,128,128]{2,1,0:T(8,128)} %bitcast.8, f32[3,128,128]{2,1,0:T(8,128)} %bitcast.9, f32[4,128,128]{2,1,0:T(8,128)} %bitcast.7, f32[3,128,128]{2,1,0:T(8,128)} %bitcast.10, s32[4,16]{1,0:T(4,128)} %bitcast.11, s32[16]{0:T(128)} %offsets_hbm.1, ...), custom_call_target="tpu_custom_call" | custom-call | tf_op jit(solution)/shard_map/pallas_call | solution.py:492
  47.3 1.8 %shard_map.168 = (f32[3,128,128]{2,1,0:T(8,128)}, f32[4,128,128]{2,1,0:T(8,128)}) custom-call(f32[3,128,128]{2,1,0:T(8,128)} %get-tuple-element.6.les_from, f32[4,128,128]{2,1,0:T(8,128)} %get-tuple-element.7.caa_from), custom_call_target="tpu_custom_call" | custom-call | tf_op jit(solution)/shard_map/pallas_call | solution.py:541

commit v4 on v3

--- a/solution.py
+++ b/solution.py
@@ -374,18 +374,17 @@
             change += les_metric[2] * across[3 + i] + u[2] * slopes[2][i]
             les_out[i] = u[i] - (0.5 * les_step) * change
 
-    def substep(k, fresh):
+    rings = (pl.ds(sector - 1, radial, stride=sector), pl.ds(0, radial, stride=sector))
+
+    def send_rows(k, way, p, v, m):
+        caa_az_send[k, way, 0:radial] = p
+        caa_az_send[k, way, radial : 2 * radial] = v
+        caa_az_send[k, way, 2 * radial : 3 * radial] = swap_azimuth(m)
+        caa_copies(k)[way].start()
+
+    def substep(k, fresh, last):
         w = [caa_out[c] for c in range(4)]
         m = margin[...]
-        for way, at in ((0, sector - 1), (1, 0)):
-            ring = pl.ds(at, radial, stride=sector)
-            caa_az_send[k, way, 0:radial] = caa_out[0, ring, :]
-            caa_az_send[k, way, radial : 2 * radial] = caa_out[2, ring, :]
-            caa_az_send[k, way, 2 * radial : 3 * radial] = swap_azimuth(margin[ring, :])
-        copies = caa_copies(k)
-        for copy in copies:
-            copy.start()
-
         high, low = split(jnp.concatenate(w, axis=0))
         m_high, m_low = split(m)
         along = product(jnp.concatenate([high, low, high], axis=1), stream_mat[...])
@@ -393,20 +392,20 @@
         fix = product(jnp.concatenate([m_high, m_low], axis=1), jnp.concatenate([table, table], axis=0))
         along = [caa_metric[0] * (along[i * rows : (i + 1) * rows] + b) for i, b in enumerate(pieces(fix, 4))]
         parts = [m_high, m_low, m_high]
+        w_high = [high[c * rows : (c + 1) * rows] for c in range(4)]
+        w_low = [low[c * rows : (c + 1) * rows] for c in range(4)]
         for c in range(4):
-            parts += [high[c * rows : (c + 1) * rows], low[c * rows : (c + 1) * rows]]
+            parts += [w_high[c], w_low[c]]
         m_along = product(jnp.concatenate(parts, axis=1), margin_mat[...])
-        around = pieces(left_apply(wide(azimuth_mat, rows), [w[0], w[2], swap_azimuth(m)]), 3)
-        across = pieces(left_apply(wide(radial_mat, rows), [w[0], w[3], swap_radial(m)]), 3)
-
-        for copy in copies:
-            copy.wait_recv()
-        rim = [
-            jnp.concatenate([caa_az_recv[k, way, c * radial : (c + 1) * radial] for way in range(2)], axis=0)
-            for c in range(3)
-        ]
-        fix = pieces(azimuth_fix(azimuth_ghost[...], jnp.concatenate(rim, axis=1)), 3)
-        around = [a + b for a, b in zip(around, fix)]
+
+        def across_rows(matrix, c, swapped):
+            s_high, s_low = split(swapped)
+            top = jnp.concatenate([w_high[0], w_high[c], s_high], axis=1)
+            under = jnp.concatenate([w_low[0], w_low[c], s_low], axis=1)
+            return pieces(product(wide(matrix, rows), jnp.concatenate([top, under, top], axis=0)), 3)
+
+        around = across_rows(azimuth_mat, 2, swap_azimuth(m))
+        across = across_rows(radial_mat, 3, swap_radial(m))
         rates = [
             mach_number * along[0] + along[1] + caa_metric[1] * around[1] + caa_metric[2] * across[1],
             mach_number * along[1] + along[0] - source[0:rows],
@@ -420,8 +419,23 @@
         rate = margin_metric[0] * m_along + margin_metric[1] * around[2] + margin_metric[2] * across[2]
         margin[...] = m - caa_step * (rate - margin_source[...])
 
+        copies = caa_copies(k)
+        for way in range(2):
+            copies[way].wait_recv()
+            ring = rings[1 - way]
+            scale = (3.0 * caa_step) * (1.0 - 2.0 * way)
+            halo = [caa_az_recv[k, way, c * radial : (c + 1) * radial] for c in range(3)]
+            p = caa_out[0, ring, :] + scale * caa_metric[1, ring, :] * halo[1]
+            v = caa_out[2, ring, :] + scale * caa_metric[1, ring, :] * halo[0]
+            edge = margin[ring, :] + scale * margin_metric[1, ring, :] * halo[2]
+            caa_out[0, ring, :] = p
+            caa_out[2, ring, :] = v
+            margin[ring, :] = edge
+            if not last:
+                send_rows(k + 1, 1 - way, p, v, edge)
+
     def later_substep(k, carry):
-        substep(k, None)
+        substep(k, None, False)
         return carry
 
     for k in range(LES_STEPS):
@@ -443,8 +457,13 @@
             for c in range(3):
                 margin_metric[c] = spread_metric[c]
         margin[...] = take_margin(1 + 2 * k)
-        substep(k * CAA_SUB, 2 + 2 * k)
-        lax.fori_loop(k * CAA_SUB + 1, (k + 1) * CAA_SUB, later_substep, 0)
+        begin = k * CAA_SUB
+        for way in range(2):
+            ring = rings[way]
+            send_rows(begin, way, caa_out[0, ring, :], caa_out[2, ring, :], margin[ring, :])
+        substep(begin, 2 + 2 * k, False)
+        lax.fori_loop(begin + 1, begin + CAA_SUB - 1, later_substep, 0)
+        substep(begin + CAA_SUB - 1, None, True)
 
     def drain_caa(k, carry):
         for copy in caa_copies(k):

time: 49.3 us -> 47.9 us (0.972)
  Pallas kernels: 48.4 us -> 47.1 us
    pallas_call x1, Pallas kernels: 46.6 us -> 45.3 us  [body(): pl.pallas_call(functools.partial(kernel, sizes), out_shape=(jax.ShapeDtyp...]
where the time goes in v4:
time: 47.9 us; the launch traced here: 47.8 us
  Pallas kernels  47.1 us (98%)
  between operations  0.64 us (1%)
    pallas_call x1, Pallas kernels, body(): pl.pallas_call(functools.partial(kernel, sizes), out_shape=(jax.ShapeDtyp...  45.3 us
    pallas_call x1, Pallas kernels, body(): pl.pallas_call(hand_over, out_shape=tuple((jax.ShapeDtypeStruct(shape, F3...  1.79 us

profile of v4, /device:TPU:1, one launch (start us, length us, event | category | flops | bytes accessed | tf_op | source)
XLA Modules:
  0.0 47.8 jit_solution(4186676241926240430)
XLA Ops:
  0.6 45.3 %shard_map.167 = (f32[3,128,128]{2,1,0:T(8,128)}, f32[4,128,128]{2,1,0:T(8,128)}) custom-call(f32[3,128,128]{2,1,0:T(8,128)} %bitcast.8, f32[3,128,128]{2,1,0:T(8,128)} %bitcast.9, f32[4,128,128]{2,1,0:T(8,128)} %bitcast.7, f32[3,128,128]{2,1,0:T(8,128)} %bitcast.10, s32[4,16]{1,0:T(4,128)} %bitcast.11, s32[16]{0:T(128)} %offsets_hbm.1, ...), custom_call_target="tpu_custom_call" | custom-call | tf_op jit(solution)/shard_map/pallas_call | solution.py:511
  46.0 1.8 %shard_map.168 = (f32[3,128,128]{2,1,0:T(8,128)}, f32[4,128,128]{2,1,0:T(8,128)}) custom-call(f32[3,128,128]{2,1,0:T(8,128)} %get-tuple-element.6.les_from, f32[4,128,128]{2,1,0:T(8,128)} %get-tuple-element.7.caa_from), custom_call_target="tpu_custom_call" | custom-call | tf_op jit(solution)/shard_map/pallas_call | solution.py:560

commit v5 on v4

--- a/solution.py
+++ b/solution.py
@@ -56,8 +56,6 @@
     stream_mat = np.concatenate([high, high, low], axis=0)
     high, low = halves(np.kron(np.eye(radial), line_matrix(sector)))
     azimuth_mat = np.concatenate([high, high, low], axis=1)
-    high, low = halves(np.kron(line_matrix(radial), np.eye(sector)))
-    radial_mat = np.concatenate([high, high, low], axis=1)
     ghost = np.zeros((rows, 2 * radial))
     for r in range(radial):
         ghost[r * sector, r] = -3.0
@@ -77,22 +75,23 @@
     inner = np.zeros((stream, 4 * stream))
     mix = mach_number * np.eye(4)
     mix[1, 0] = mix[0, 1] = 1.0
-    joint = np.zeros((4, stream, stream))
+    joint = np.zeros((stream, stream))
     spread = np.zeros((stream, 3 * stream))
     for c in range(4):
         inner[2 * m * c + m - 1, c * stream] = -3.0
         inner[2 * m * c + m, c * stream + stream - 1] = 3.0
         for o in range(4):
-            joint[c, 0, 2 * m * o + m - 1] = 3.0 * mix[c, o]
-            joint[c, stream - 1, 2 * m * o + m] = -3.0 * mix[c, o]
+            joint[0, 2 * m * o + m - 1] = 3.0
+            joint[stream - 1, 2 * m * o + m] = -3.0
             if c < 3:
                 for t in range(2 * m):
                     spread[2 * m * c + t, c * stream + 2 * m * o + t] = 1.0
     high, low = halves(np.kron(mix, np.kron(np.eye(2), line_matrix(m).T)))
-    joint = [joint[c // 2].astype(BF16) for c in range(8)]
-    margin_mat = np.concatenate([high, high, low] + joint, axis=0)
-    columns = [azimuth_mat, radial_mat, stream_ghost, les_pick, inner.astype(BF16), spread.astype(BF16)]
-    return [stream_mat, azimuth_ghost, margin_mat] + [tall(t, stream) for t in columns]
+    margin_mat = np.concatenate([high, low], axis=0)
+    joint = joint.astype(BF16)
+    joint = np.concatenate([joint, joint, 0 * joint], axis=0)
+    columns = [azimuth_mat, stream_ghost, les_pick, inner.astype(BF16), spread.astype(BF16)]
+    return [stream_mat, azimuth_ghost, margin_mat, joint] + [tall(t, stream) for t in columns]
 
 
 def tall(table, width):
@@ -144,11 +143,11 @@
 def kernel(
     sizes,
     les_hbm, les_metric_hbm, caa_hbm, caa_metric_hbm, refs_hbm, offsets_hbm, send_list_hbm,
-    stream_mat_hbm, azimuth_ghost_hbm, margin_mat_hbm,
-    azimuth_mat_hbm, radial_mat_hbm, stream_ghost_hbm, les_pick_hbm, inner_hbm, spread_hbm,
+    stream_mat_hbm, azimuth_ghost_hbm, margin_mat_hbm, joint_hbm,
+    azimuth_mat_hbm, stream_ghost_hbm, les_pick_hbm, inner_hbm, spread_hbm,
     les_out, caa_out,
     les_in, les_metric, caa_metric, refs, offsets, send_list,
-    stream_mat, azimuth_ghost, margin_mat, azimuth_mat, radial_mat, stream_ghost, les_pick, inner, spread,
+    stream_mat, azimuth_ghost, margin_mat, joint, azimuth_mat, stream_ghost, les_pick, inner, spread,
     load_sems,
     source, weights, chooser,
     les_az_send, les_az_recv, les_st_send, les_st_recv,
@@ -178,7 +177,7 @@
             [
                 (refs_hbm, refs), (offsets_hbm, offsets), (send_list_hbm, send_list),
                 (les_hbm, les_in), (les_pick_hbm, les_pick),
-                (stream_mat_hbm, stream_mat), (azimuth_mat_hbm, azimuth_mat), (radial_mat_hbm, radial_mat),
+                (stream_mat_hbm, stream_mat), (azimuth_mat_hbm, azimuth_mat), (joint_hbm, joint),
                 (azimuth_ghost_hbm, azimuth_ghost), (stream_ghost_hbm, stream_ghost),
                 (les_metric_hbm, les_metric), (caa_hbm, caa_out), (margin_mat_hbm, margin_mat), (inner_hbm, inner), (spread_hbm, spread),
                 (caa_metric_hbm, caa_metric),
@@ -234,8 +233,9 @@
         copies = pair(les_sems, k, 0, les_az_send, les_az_recv, (above_id, below_id))
         return copies + pair(les_sems, k, 2, les_st_send, les_st_recv, (down_id, up_id))
 
-    def caa_copies(k):
-        return pair(caa_sems, k, 0, caa_az_send, caa_az_recv, (above_id, below_id))
+    def caa_copies(k, ways=(0, 1)):
+        copies = pair(caa_sems, k, 0, caa_az_send, caa_az_recv, (above_id, below_id))
+        return [copies[way] for way in ways]
 
     def margin_copies(i):
         return [
@@ -287,6 +287,16 @@
             send_sem=lamb_send_sem.at[k, d], recv_sem=lamb_recv_sem.at[k, d],
             device_id={"sec": sec, "gx": d, "az": az}, device_id_type=MESH,
         )
+
+    radial_table = line_matrix(radial)
+
+    def radial_apply(field):
+        layers = [field[i * sector : (i + 1) * sector] for i in range(radial)]
+        result = []
+        for o in range(radial):
+            terms = [float(radial_table[o, i]) * layers[i] for i in range(radial) if abs(radial_table[o, i]) > 1e-9]
+            result.append(sum(terms[1:], terms[0]))
+        return jnp.concatenate(result, axis=0)
 
     def ghosts(recv, k):
         before = jnp.where(slab > 0, recv[k, 0], 0.0)
@@ -322,7 +332,7 @@
         along = right_apply(stacked[0], stream_mat[...])
         along = [along[i * rows : (i + 1) * rows] for i in range(6)]
         around = pieces(left_apply(wide(azimuth_mat, rows), stacked[1]), 6)
-        across = pieces(left_apply(wide(radial_mat, rows), stacked[2]), 6)
+        across = [radial_apply(field) for field in stacked[2]]
 
         for copy in copies:
             copy.wait_recv()
@@ -386,26 +396,25 @@
         w = [caa_out[c] for c in range(4)]
         m = margin[...]
         high, low = split(jnp.concatenate(w, axis=0))
-        m_high, m_low = split(m)
-        along = product(jnp.concatenate([high, low, high], axis=1), stream_mat[...])
-        table = wide(inner, rows)
-        fix = product(jnp.concatenate([m_high, m_low], axis=1), jnp.concatenate([table, table], axis=0))
-        along = [caa_metric[0] * (along[i * rows : (i + 1) * rows] + b) for i, b in enumerate(pieces(fix, 4))]
-        parts = [m_high, m_low, m_high]
+        m_high = m.astype(BF16)
+        both = product(
+            jnp.concatenate([high, low, high], axis=1), jnp.concatenate([stream_mat[...], joint[...]], axis=1)
+        )
+        fix = pieces(product(m_high, wide(inner, rows)), 4)
+        along = [caa_metric[0] * (both[c * rows : (c + 1) * rows, 0:stream] + fix[c]) for c in range(4)]
+        edges = [both[c * rows : (c + 1) * rows, stream : 2 * stream] for c in range(4)]
+        partner = jnp.where(group == 0, edges[1], jnp.where(group == 1, edges[0], 0.0))
+        own = jnp.where(group < 2, jnp.where(group == 0, edges[0], edges[1]), jnp.where(group == 2, edges[2], edges[3]))
+        m_along = product(jnp.concatenate([m_high, m_high], axis=1), margin_mat[...]) + (mach_number * own + partner)
         w_high = [high[c * rows : (c + 1) * rows] for c in range(4)]
         w_low = [low[c * rows : (c + 1) * rows] for c in range(4)]
-        for c in range(4):
-            parts += [w_high[c], w_low[c]]
-        m_along = product(jnp.concatenate(parts, axis=1), margin_mat[...])
-
-        def across_rows(matrix, c, swapped):
-            s_high, s_low = split(swapped)
-            top = jnp.concatenate([w_high[0], w_high[c], s_high], axis=1)
-            under = jnp.concatenate([w_low[0], w_low[c], s_low], axis=1)
-            return pieces(product(wide(matrix, rows), jnp.concatenate([top, under, top], axis=0)), 3)
-
-        around = across_rows(azimuth_mat, 2, swap_azimuth(m))
-        across = across_rows(radial_mat, 3, swap_radial(m))
+        table = wide(azimuth_mat, rows)
+        top = jnp.concatenate([w_high[0], w_high[2]], axis=1)
+        under = jnp.concatenate([w_low[0], w_low[2]], axis=1)
+        around = pieces(product(table, jnp.concatenate([top, under, top], axis=0)), 2)
+        swapped = swap_azimuth(m).astype(BF16)
+        around.append(product(table[:, rows : 3 * rows], jnp.concatenate([swapped, swapped], axis=0)))
+        across = [radial_apply(field) for field in (w[0], w[3], swap_radial(m))]
         rates = [
             mach_number * along[0] + along[1] + caa_metric[1] * around[1] + caa_metric[2] * across[1],
             mach_number * along[1] + along[0] - source[0:rows],

time: 47.9 us -> 47.9 us (level)
  no operation moved by 1% of the time
where the time goes in v5:
time: 47.9 us; the launch traced here: 47.7 us
  Pallas kernels  47.1 us (98%)
  between operations  0.64 us (1%)
    pallas_call x1, Pallas kernels, body(): pl.pallas_call(functools.partial(kernel, sizes), out_shape=(jax.ShapeDtyp...  45.3 us
    pallas_call x1, Pallas kernels, body(): pl.pallas_call(hand_over, out_shape=tuple((jax.ShapeDtypeStruct(shape, F3...  1.79 us

profile of v5, /device:TPU:1, one launch (start us, length us, event | category | flops | bytes accessed | tf_op | source)
XLA Modules:
  0.0 47.7 jit_solution(6676652605835207588)
XLA Ops:
  0.6 45.3 %shard_map.167 = (f32[3,128,128]{2,1,0:T(8,128)}, f32[4,128,128]{2,1,0:T(8,128)}) custom-call(f32[3,128,128]{2,1,0:T(8,128)} %bitcast.8, f32[3,128,128]{2,1,0:T(8,128)} %bitcast.9, f32[4,128,128]{2,1,0:T(8,128)} %bitcast.7, f32[3,128,128]{2,1,0:T(8,128)} %bitcast.10, s32[4,16]{1,0:T(4,128)} %bitcast.11, s32[16]{0:T(128)} %offsets_hbm.1, ...), custom_call_target="tpu_custom_call" | custom-call | tf_op jit(solution)/shard_map/pallas_call | solution.py:520
  45.9 1.8 %shard_map.168 = (f32[3,128,128]{2,1,0:T(8,128)}, f32[4,128,128]{2,1,0:T(8,128)}) custom-call(f32[3,128,128]{2,1,0:T(8,128)} %get-tuple-element.6.les_from, f32[4,128,128]{2,1,0:T(8,128)} %get-tuple-element.7.caa_from), custom_call_target="tpu_custom_call" | custom-call | tf_op jit(solution)/shard_map/pallas_call | solution.py:569
